TPU v7x, 128 devices: a whole 4x4x4 slice. The times are simulated.
128 devices in a mesh: cat: 4 (over z), row: 2 (over x_hi), loop: 16 (over x_lo, y, core).
Axes of the slice: x: 4 (x_hi: 2, x_lo: 2; x = x_hi * 2 + x_lo), y: 4, z: 4, core: 2. Of those that a mesh axis runs over, the one named last changes fastest.
Arguments:
- queries: bfloat16 [65536, 512], P(('cat', 'row', 'loop')), may hold values from -60 to 60
- categories: int32 [65536, 1], P(('cat', 'row', 'loop')), may hold values from 0 to 3; in each aligned block of 512 rows (0 to 511, 512 to 1023, ...) at most 256 rows name the same one
- item_keys: bfloat16 [32768, 512], P(('cat', 'row', 'loop')), may hold values from -40 to 40
- item_values: bfloat16 [32768, 512], P(('cat', 'row', 'loop')), may hold values from -6 to 6
Outputs:
- soft_targets: bfloat16 [65536, 512], P(('cat', 'row', 'loop'))
Inputs may be any that keep to these rules, and one draw needn't show every extreme that they name: `categories`: in the 512 rows of one device no category appears more than 256 times.
All inputs are finite; a program needn't handle non-finite values.
Results may differ from a plain program's by a relative error of at most 0.024.
Values may be sent and summed in bfloat16 or wider, within the bound.
No kernel may reach another device: no remote copies, remote signals or barrier semaphores. Data moves between devices by JAX's collectives and lax.ppermute only.
A program may use at most 128 MiB of HBM per device.

v0:
```python
import math

import jax
import jax.numpy as jnp
from jax import lax
from jax.sharding import PartitionSpec as P

D = 512
CAP = 256


def start_state(slot_count, feat_width):
    return (
        jnp.full((slot_count,), -1e30, jnp.float32),
        jnp.zeros((slot_count,), jnp.float32),
        jnp.zeros((slot_count, feat_width), jnp.float32),
    )


def make_fold(block_query, state_tuple, item_piece):
    score_scale = 1.4 / math.sqrt(D)
    running_max, running_sum, weighted = state_tuple
    key_piece, value_piece = item_piece
    scores = (
        lax.dot_general(
            block_query, key_piece, (((1,), (1,)), ((), ())), preferred_element_type=jnp.float32
        )
        * score_scale
    )
    new_max = jnp.maximum(running_max, jnp.max(scores, axis=1))
    expo = jnp.exp(scores - new_max[:, None])
    running_sum = jnp.sum(expo, axis=1)
    weighted = jnp.dot(expo.astype(jnp.bfloat16), value_piece, preferred_element_type=jnp.float32)
    return (new_max, running_sum, weighted)


def shards(queries, categories, item_keys, item_values):
    row_count, feat_width = queries.shape
    groups = lax.axis_size("cat")
    cat_ids = categories[:, 0]
    onehot = (cat_ids[:, None] == jnp.arange(groups, dtype=jnp.int32)[None, :]).astype(jnp.int32)
    slot_rank = jnp.sum(jnp.cumsum(onehot, axis=0) * onehot, axis=1) - 1
    slot_index = cat_ids * CAP + slot_rank
    outgoing = jnp.zeros((groups * CAP, feat_width), jnp.bfloat16).at[slot_index].set(queries)
    arrived = lax.all_to_all(
        outgoing.reshape(groups, CAP, feat_width), "cat", split_axis=0, concat_axis=0, tiled=True
    ).reshape(groups * CAP, feat_width)
    slot_count = groups * CAP
    state = make_fold(
        arrived,
        start_state(slot_count, feat_width),
        (
            lax.all_gather(item_keys, ("row", "loop"), axis=0, tiled=True),
            lax.all_gather(item_values, ("row", "loop"), axis=0, tiled=True),
        ),
    )
    pooled = state[2] / state[1][:, None]
    normed = (pooled * lax.rsqrt(jnp.mean(pooled * pooled, axis=1, keepdims=True) + 1e-06)).astype(
        jnp.bfloat16
    )
    returned = lax.all_to_all(
        normed.reshape(groups, CAP, feat_width), "cat", split_axis=0, concat_axis=0, tiled=True
    ).reshape(groups * CAP, feat_width)
    return returned[slot_index]


def solution(mesh):
    placed = (
        P(("cat", "row", "loop"), None),
        P(("cat", "row", "loop"), None),
        P(("cat", "row", "loop"), None),
        P(("cat", "row", "loop"), None),
    )
    return jax.shard_map(
        shards,
        mesh=mesh,
        in_specs=placed,
        out_specs=P(("cat", "row", "loop"), None),
        check_vma=False,
    )
```

profile of v0, /device:TPU:1, one launch (start us, length us, event | category | flops | bytes accessed | tf_op | source)
XLA Modules:
  0.0 168.0 jit_solution(7036646173567159412)
XLA Ops:
  6.5 0.0 all-gather.3.cloned.1.call-start
  6.5 0.7 all-gather.3.cloned.1.call-update
  7.3 0.0 all-gather.5.cloned.1.call-start
  7.3 0.7 all-gather.5.cloned.1.call-update
  8.0 0.7 fusion.13
  8.7 1.2 reduce-window.6
  9.9 0.2 slice_reduce_fusion
  10.1 0.2 reduce-window.9
  10.3 0.1 add_bitcast_fusion
  10.4 0.7 fusion.12
  11.1 0.7 compare_select_fusion
  11.8 3.2 %scatter_custom_fusion = bf16[1024,512]{1,0:T(8,128)(2,1)S(1)} fusion(s32[512]{0:T(512)S(1)} %bitcast.31, bf16[512,512]{1,0:T(8,128)(2,1)} %param.4, bf16[]{:T(256)} %constant.11.clone.1), kind=kCustom, calls=%fused_computation.12 | custom fusion | bytes 1049088 | tf_op jit(solution)/shard_map/scatter | solution.py:44
  15.0 19.8 %all_to_all.10 = bf16[4,256,512]{2,1,0:T(8,128)(2,1)S(1)} all-to-all(bf16[4,256,512]{2,1,0:T(8,128)(2,1)S(1)} %bitcast.27), channel_id=1, replica_groups=mesh['cat'=4,'row'=2,'loop'=16] {'cat'}, dimensions={0} | all-to-all | bytes 2097152 | tf_op jit(solution)/shard_map/all_to_all | solution.py:45
  34.9 31.2 %all-gather.3.cloned.1.call-done = bf16[8192,512]{1,0:T(8,128)(2,1)} async-done(((bf16[256,512]{1,0:T(8,128)(2,1)}), bf16[8192,512]{1,0:T(8,128)(2,1)}) %all-gather.3.cloned.1.call-update) | async-done | bytes 8388624 | tf_op jit(solution)/shard_map/all_gather | solution.py:53
  66.0 19.0 %multiply_reduce_fusion = (f32[1024]{0:T(1024)S(1)}, f32[1024,8192]{1,0:T(8,128)}) fusion(bf16[1024,512]{1,0:T(8,128)(2,1)S(1)} %bitcast.28, bf16[8192,512]{1,0:T(8,128)(2,1)} %all-gather.3.cloned.1.call-done), kind=kOutput, calls=%fused_computation.3 | convolution fusion | flops 8606710784 | bytes 42995712 | tf_op jit(solution)/shard_map/dot_general | solution.py:25
  85.1 14.1 %fusion = f32[1024]{0:T(1024)S(1)} fusion(f32[1024,8192]{1,0:T(8,128)} %get-tuple-element.6, f32[1024]{0:T(1024)S(1)} %broadcast_maximum_fusion), kind=kLoop, calls=%fused_computation.4 | loop fusion | flops 25164800 | bytes 33562624 | tf_op jit(solution)/shard_map/reduce_sum | solution.py:32
  99.2 21.5 %all-gather.5.cloned.1.call-done = bf16[8192,512]{1,0:T(8,128)(2,1)} async-done(((bf16[256,512]{1,0:T(8,128)(2,1)}), bf16[8192,512]{1,0:T(8,128)(2,1)}) %all-gather.5.cloned.1.call-update) | async-done | bytes 8388624 | tf_op jit(solution)/shard_map/all_gather | solution.py:54
  120.7 17.8 %multiply_reduce_fusion.1 = (f32[1024]{0:T(1024)S(1)}, f32[1024,512]{1,0:T(8,128)S(1)}) fusion(f32[1024]{0:T(1024)S(1)} %fusion, bf16[8192,512]{1,0:T(8,128)(2,1)} %all-gather.5.cloned.1.call-done, f32[1024,8192]{1,0:T(8,128)} %get-tuple-element.6, f32[1024]{0:T(1024)S(1)} %broadcast_maximum_fusion), kind=kOutput, calls=%fused_computation.10 | convolution fusion | flops 8616672256 | bytes 44052480 | tf_op jit(solution)/shard_map/dot_general | solution.py:33
  138.5 1.2 multiply_convert_fusion
  139.7 4.1 %all-to-all-start.1 = ((bf16[4,256,512]{2,1,0:T(8,128)(2,1)}), bf16[4,256,512]{2,1,0:T(8,128)(2,1)S(1)}, u32[]{:S(2)}, u32[]{:S(2)}) async-start(bf16[4,256,512]{2,1,0:T(8,128)(2,1)} %bitcast.7), calls=%async_computation.1 | async-start | bytes 2097152 | tf_op jit(solution)/shard_map/all_to_all | solution.py:61
  143.9 14.7 %all-to-all-done.1 = bf16[4,256,512]{2,1,0:T(8,128)(2,1)S(1)} async-done(((bf16[4,256,512]{2,1,0:T(8,128)(2,1)}), bf16[4,256,512]{2,1,0:T(8,128)(2,1)S(1)}, u32[]{:S(2)}, u32[]{:S(2)}) %all-to-all-start.1) | async-done | bytes 1048608 | tf_op jit(solution)/shard_map/all_to_all | solution.py:61
  158.6 2.6 %gather_fusion = bf16[512,512]{1,0:T(8,128)(2,1)} fusion(bf16[1024,512]{1,0:T(8,128)(2,1)S(1)} %bitcast.26, s32[1024]{0:T(1024)S(1)} %pad_clamp_fusion), kind=kCustom, calls=%fused_computation | custom fusion | bytes 1050624 | tf_op jit(solution)/shard_map/gather | solution.py:64
  (4 shorter events, 0.0 us)
Async XLA Ops:
  6.5 59.5 %all-gather.3.cloned.1.call-start = ((), (), s32[]{:S(2)}) async-start(), calls=%async_computation.2 | async-start | bytes 8650752 | tf_op jit(solution)/shard_map/all_gather | solution.py:53
  7.3 113.5 %all-gather.5.cloned.1.call-start = ((), (), s32[]{:S(2)}) async-start(), calls=%async_computation.3 | async-start | bytes 8650752 | tf_op jit(solution)/shard_map/all_gather | solution.py:54
  139.7 18.8 %all-to-all-start.1 = ((bf16[4,256,512]{2,1,0:T(8,128)(2,1)}), bf16[4,256,512]{2,1,0:T(8,128)(2,1)S(1)}, u32[]{:S(2)}, u32[]{:S(2)}) async-start(bf16[4,256,512]{2,1,0:T(8,128)(2,1)} %bitcast.7), calls=%async_computation.1 | async-start | bytes 2097152 | tf_op jit(solution)/shard_map/all_to_all | solution.py:61
Sparse Core Ops, SparseCore 0:
  9.6 56.3 all-gather.2
  68.3 52.3 all-gather.4
where the time goes:
time: 168 us
  waiting for transfers between devices  68.8 us (41%)
  matrix products  36.8 us (22%)
  blocking collectives  19.8 us (12%)
  other arithmetic  18.9 us (11%)
  between operations  13.4 us (8%)
  local copies, waits for them, and re-layouts  6.05 us (4%)
  starting transfers between devices  4.18 us (2%)
    all_gather x1, waiting for transfers between devices, shards(): lax.all_gather(item_keys, ('row', 'loop'), axis=0, tiled=True)  31.2 us
    all_gather x1, waiting for transfers between devices, shards(): lax.all_gather(item_values, ('row', 'loop'), axis=0, tiled=True)  21.5 us
    all_to_all x1, blocking collectives, shards(): lax.all_to_all(outgoing.reshape(groups, CAP, feat_width), 'cat', split_ax...  19.8 us
    dot_general x1, matrix products, make_fold(): lax.dot_general(block_query, key_piece, (((1,), (1,)), ((), ())), preferr...  19 us
    dot_general x1, matrix products, make_fold(): jnp.dot(expo.astype(jnp.bfloat16), value_piece, preferred_element_type=jn...  17.8 us
    all_to_all x1, waiting for transfers between devices, shards(): lax.all_to_all(normed.reshape(groups, CAP, feat_width), 'cat', split_axis...  14.7 us
    reduce_sum x1, other arithmetic, make_fold(): running_sum = jnp.sum(expo, axis=1)  14.1 us
    all_to_all x1, starting transfers between devices, shards(): lax.all_to_all(normed.reshape(groups, CAP, feat_width), 'cat', split_axis...  4.14 us
  transfers between devices with their start and end apart: 3, of which 3 were waited for; matrix products, arithmetic and copies ran while one was open for 24% of the time, Pallas kernels for 0%

commit v1 on v0

v1 whole, which is shorter than its diff:
```python
import functools
import math

import jax
import jax.numpy as jnp
from jax import lax
from jax.experimental import pallas as pl
from jax.experimental.pallas import tpu as pltpu
from jax.sharding import PartitionSpec as P

D = 512
CAP = 256
CATS = 4
BLOCK = 256
SCALE = 1.4 / math.sqrt(D) * math.log2(math.e)
BF = jnp.bfloat16
F32 = jnp.float32
PLANE = ("row", "loop")
VMEM = pl.BlockSpec(memory_space=pltpu.VMEM)


def place(x, y, core):
    return ((x % 4) * 4 + y % 4) * 2 + core


def hops(first, step):
    pairs = []
    for x in range(4):
        for y in range(4):
            for core in range(2):
                along_x = (core == 0) == first
                to = place(x + step, y, core) if along_x else place(x, y + step, core)
                pairs.append((place(x, y, core), to))
    return pairs


def first_hop(a, step):
    return lax.ppermute(a, PLANE, hops(True, step))


def second_hop(a, step):
    return lax.ppermute(a, PLANE, hops(False, step))


def swap_cores(a):
    return lax.ppermute(a, PLANE, [(i, i ^ 1) for i in range(32)])


def plane_hop(a, step):
    pairs = []
    for cat in range(CATS):
        for i in range(32):
            to = (cat + (step if i % 2 == 0 else -step)) % CATS
            pairs.append((cat * 32 + i, to * 32 + i))
    return lax.ppermute(a, ("cat",) + PLANE, pairs)


def opposite_plane(a):
    return lax.ppermute(a, "cat", [(i, (i + 2) % CATS) for i in range(CATS)])


def after(a, *earlier):
    return lax.optimization_barrier((a, *earlier))[0]


def nt(a, b):
    return lax.dot_general(a, b, (((1,), (1,)), ((), ())), preferred_element_type=F32)


def nn(a, b):
    return jnp.dot(a, b, preferred_element_type=F32)


def params(mib):
    return pltpu.CompilerParams(vmem_limit_bytes=mib * 1024 * 1024)


def classes(cats):
    rows = cats.shape[1]
    ahead = cats - lax.axis_index("cat")
    rel = jnp.where(lax.axis_index("loop") % 2 == 0, ahead, -ahead) & (CATS - 1)
    named = lax.broadcasted_iota(jnp.int32, (16, rows), 0) == rel
    before = lax.broadcasted_iota(jnp.int32, (rows, rows), 0) < lax.broadcasted_iota(
        jnp.int32, (rows, rows), 1
    )
    rank = nn(named.astype(BF), before.astype(BF))
    rank = jnp.sum(jnp.where(named, rank, 0.0), axis=0, keepdims=True)
    return rel * CAP + rank.astype(jnp.int32)


def dispatch_kernel(cat_ref, far_cat_ref, q_ref, far_q_ref, out0, sent, far0, slot_ref):
    rows = cat_ref.shape[1]
    slot, far_slot = classes(cat_ref[...]), classes(far_cat_ref[...])
    iota = lax.broadcasted_iota(jnp.int32, (CAP, rows), 0)

    def pick(r, slots, ref):
        return nn((iota + r * CAP == slots).astype(BF), ref[...]).astype(BF)

    sent[0:CAP, :] = pick(1, slot, q_ref)
    sent[CAP : 2 * CAP, :] = pick(1, far_slot, far_q_ref)
    sent[2 * CAP : 3 * CAP, :] = pick(2, slot, q_ref)
    out0[...] = pick(0, slot, q_ref)
    far0[...] = pick(0, far_slot, far_q_ref)
    column = jnp.transpose(jnp.broadcast_to(slot.astype(F32), (128, rows)))
    slot_ref[...] = column.astype(jnp.int32)


def dispatch(cats, far_cats, queries, far_queries):
    rows = queries.shape[0]
    out = lambda n: jax.ShapeDtypeStruct((n, D), BF)
    return pl.pallas_call(
        dispatch_kernel,
        out_shape=[out(CAP), out(3 * CAP), out(CAP)]
        + [jax.ShapeDtypeStruct((rows, 128), jnp.int32)],
        in_specs=[VMEM] * 4,
        out_specs=[VMEM] * 4,
        compiler_params=params(16),
    )(cats, far_cats, queries, far_queries)


def softmax_tile(scores, values, old):
    m = jnp.max(functools.reduce(jnp.maximum, scores), axis=1, keepdims=True)
    if old is not None:
        m = jnp.maximum(m, old[0])
    es = [jnp.exp2((s - m) * SCALE) for s in scores]
    l = jnp.sum(functools.reduce(jnp.add, es), axis=1, keepdims=True)
    o = functools.reduce(jnp.add, [nn(e.astype(BF), v) for e, v in zip(es, values)])
    if old is not None:
        back = jnp.exp2((old[0] - m) * SCALE)
        l = l + old[1] * back
        o = o + old[2] * back
    return m, l, o


def parts_of(x):
    high = x.astype(BF)
    rest = x - high.astype(F32)
    middle = rest.astype(BF)
    return high, middle, (rest - middle.astype(F32)).astype(BF)


def two_lanes(m, l):
    lane = lax.broadcasted_iota(jnp.int32, (m.shape[0], 128), 1)
    return jnp.where(lane == 0, m, l)


def fold_kernel(plan, tiles, groups, inputs, packed, *refs):
    n_items, n_qs, has_state = inputs
    items, qs, rest = refs[:n_items], refs[n_items : n_items + n_qs], list(refs[n_items + n_qs :])
    states = []
    if has_state:
        states = [(rest.pop(0), rest.pop(0)) for _ in range(groups)]
    outs = rest
    jobs = []
    for i, (blocks, begin) in enumerate(plan):
        if blocks:
            jobs.append((i // CATS, i % CATS, tiles[i], blocks, begin))

    def score(job):
        ref, row = job[2]
        q = qs[ref][pl.ds(row, CAP), :]
        return [nt(q, items[a][pl.ds(b, BLOCK), :]) for a, b, _, _ in job[3]]

    scores = score(jobs[0])
    for n, (group, t, _, blocks, begin) in enumerate(jobs):
        ahead = score(jobs[n + 1]) if n + 1 < len(jobs) else None
        values = [items[c][pl.ds(d, BLOCK), :] for _, _, c, d in blocks]
        rows = pl.ds(t * CAP, CAP)
        old = None
        if not begin:
            acc, ml = states[group]
            old = (ml[rows, 0:1], ml[rows, 1:2], acc[rows, :])
        m, l, o = softmax_tile(scores, values, old)
        if packed:
            (out,) = outs
            out[rows, 0:D] = (o * (1.0 / l)).astype(BF)
            lane = lax.broadcasted_iota(jnp.int32, (CAP, 128), 1)
            extra = jnp.zeros((CAP, 128), F32)
            for i, part in enumerate(parts_of(m) + parts_of(l)):
                extra = jnp.where(lane == i, part.astype(F32), extra)
            out[rows, D : D + 128] = extra.astype(BF)
        else:
            acc, ml = outs[2 * group : 2 * group + 2]
            acc[rows, :] = o
            ml[rows, :] = two_lanes(m, l)
        scores = ahead


def fold(qs, tiles, items, plan, states, packed=False, weight=1):
    groups = len(tiles) // CATS
    flat = [a for s in states or () for a in s]
    args = [*items, *qs, *flat]
    rows = CATS * CAP
    aliases = {}
    if packed:
        out_shape = [jax.ShapeDtypeStruct((rows, D + 128), BF)]
    else:
        out_shape = [
            jax.ShapeDtypeStruct((rows, D), F32),
            jax.ShapeDtypeStruct((rows, 128), F32),
        ] * groups
        aliases = {len(args) - len(flat) + i: i for i in range(len(flat))}
    work = int(sum(len(blocks) for blocks, _ in plan) * CAP * BLOCK * weight)
    kernel = functools.partial(
        fold_kernel, plan, tiles, groups, (len(items), len(qs), states is not None), packed
    )
    out = pl.pallas_call(
        kernel,
        out_shape=out_shape,
        in_specs=[VMEM] * len(args),
        out_specs=[VMEM] * len(out_shape),
        input_output_aliases=aliases,
        compiler_params=params(24),
        cost_estimate=pl.CostEstimate(
            flops=4 * work * D, bytes_accessed=len(items) * BLOCK * D, transcendentals=work
        ),
    )(*args)
    return out[0] if packed else [tuple(out[2 * g : 2 * g + 2]) for g in range(groups)]


def merge_kernel(acc, ml, other, acc_out, ml_out):
    for t in range(CATS):
        rows = pl.ds(t * CAP, CAP)
        extra = other[rows, D : D + 128].astype(F32)
        m_own, l_own = ml[rows, 0:1], ml[rows, 1:2]
        m_far = extra[:, 0:1] + extra[:, 1:2] + extra[:, 2:3]
        l_far = extra[:, 3:4] + extra[:, 4:5] + extra[:, 5:6]
        m = jnp.maximum(m_own, m_far)
        w_own = jnp.exp2((m_own - m) * SCALE)
        w_far = jnp.exp2((m_far - m) * SCALE) * l_far
        acc_out[rows, :] = acc[rows, :] * w_own + other[rows, 0:D].astype(F32) * w_far
        ml_out[rows, :] = two_lanes(m, l_own * w_own + w_far)


def merge(state, other):
    return pl.pallas_call(
        merge_kernel,
        out_shape=[jax.ShapeDtypeStruct(a.shape, a.dtype) for a in state],
        in_specs=[VMEM] * 3,
        out_specs=[VMEM] * 2,
        input_output_aliases={0: 0, 1: 1},
        compiler_params=params(16),
    )(*state, other)


def finish_kernel(tiles, count, *refs):
    qs, stacks, (acc, ml, *outs) = refs[:4], refs[4 : 4 + count], refs[4 + count :]
    keys = [a[0:BLOCK, :] for a in stacks]
    values = [a[BLOCK : 2 * BLOCK, :] for a in stacks]

    def score(t):
        ref, row = tiles[t]
        q = qs[ref][pl.ds(row, CAP), :]
        return [nt(q, k) for k in keys]

    scores = score(0)
    for t in range(CATS):
        ahead = score(t + 1) if t + 1 < CATS else None
        rows = pl.ds(t * CAP, CAP)
        _, l, o = softmax_tile(scores, values, (ml[rows, 0:1], ml[rows, 1:2], acc[rows, :]))
        inverse = 1.0 / l
        mean = jnp.mean(o * o, axis=1, keepdims=True) * inverse * inverse
        outs[t][...] = (o * (inverse * lax.rsqrt(mean + 1e-06))).astype(BF)
        scores = ahead


def finish(qs, tiles, blocks, state):
    return pl.pallas_call(
        functools.partial(finish_kernel, tiles, len(blocks)),
        out_shape=[jax.ShapeDtypeStruct((CAP, D), BF)] * CATS,
        in_specs=[VMEM] * (6 + len(blocks)),
        out_specs=[VMEM] * CATS,
        compiler_params=params(16),
    )(*qs, *blocks, *state)


def collect_kernel(slot_ref, r0, r1, r2, r3, out):
    rows = slot_ref.shape[0]
    slot = jnp.concatenate([slot_ref[...]] * 2, axis=1)
    lane = lax.broadcasted_iota(jnp.int32, (rows, CAP), 1)
    total = None
    for r, ref in enumerate((r0, r1, r2, r3)):
        pick = (lane + r * CAP == slot).astype(BF)
        part = nn(pick, ref[0:CAP, :])
        total = part if total is None else total + part
    out[...] = total.astype(BF)


def collect(slots, returned):
    rows = slots.shape[0]
    return pl.pallas_call(
        collect_kernel,
        out_shape=jax.ShapeDtypeStruct((rows, D), BF),
        in_specs=[VMEM] * 5,
        out_specs=VMEM,
        compiler_params=params(16),
    )(slots, *returned)


def shards(queries, categories, item_keys, item_values):
    rows = queries.shape[0]
    cats = categories.reshape(1, rows)
    q0, sent, far_q0, slots = dispatch(cats, swap_cores(cats), queries, swap_cores(queries))
    here = jnp.concatenate([item_keys, item_values], axis=0)
    left, right = first_hop(here, 1), first_hop(here, -1)
    q12 = after(plane_hop(sent, 1), left, right)
    q2 = plane_hop(q12[2 * CAP :], 1)
    far_q12, far_q2 = swap_cores(q12), swap_cores(q2)
    early = [q0, q12, far_q0, far_q12]
    qs = early + [q2, far_q2]
    own = ((0, 0), (1, 0), (3, CAP), (4, 0))
    theirs = ((2, 0), (3, 0), (1, CAP), (5, 0))
    tiles = own + theirs

    pair = after(jnp.concatenate([left, right], axis=0), slots)
    up_pair, down_pair = second_hop(pair, 1), second_hop(pair, -1)
    far = first_hop(left, 1)
    whole = lambda i, j=0: (i, j, i, j + BLOCK)
    two = 2 * BLOCK

    def same(blocks):
        return ((tuple(blocks), False),) * (2 * CATS)

    first = tuple(whole(i) for i in range(3))
    plan = (((first, True),) * 3 + (((), True),)) * 2
    state = fold(early, tiles, [here, left, right], plan, None, weight=1)
    rest = jnp.concatenate([here, after(far, state[0][1])], axis=0)
    up_rest, down_rest = second_hop(rest, 1), second_hop(rest, -1)
    own_far = whole(3)
    plan = ((((own_far,), False),) * 3 + ((first + (own_far,), True),)) * 2
    state = fold(qs, tiles, [here, left, right, far], plan, state, weight=1)
    up_left = second_hop(after(up_pair[:two], state[0][1]), 1)
    down_right = second_hop(after(down_pair[two:], state[0][1]), -1)
    both = same([whole(i, j) for i in range(2) for j in (0, two)])
    state = fold(qs, tiles, [up_pair, down_pair], both, state, weight=1)
    up_here = second_hop(up_rest[:two], 1)
    down_far = second_hop(down_rest[two:], -1)
    mine, others = fold(qs, tiles, [up_rest, down_rest], both, state, weight=1)
    tail = [after(up_left, up_here, down_far), down_right]
    last_plan = same([whole(0), whole(1)])[:CATS]
    other = swap_cores(fold(qs, theirs, tail, last_plan, [others], True, weight=1))
    (mine,) = fold(qs, own, tail, last_plan, [mine], weight=1)
    merged = merge(mine, other)
    last = [up_here, down_far]
    last += [swap_cores(a) for a in last]
    mine_q = ((0, 0), (1, 0), (2, CAP), (3, 0))
    done = finish([q0, q12, far_q12, q2], mine_q, last, merged)
    back2 = opposite_plane(done[3])
    ahead, behind = plane_hop(done[1], -1), plane_hop(done[2], 1)
    return collect(slots, (done[0], ahead, back2, behind))


def solution(mesh):
    placed = P(("cat", "row", "loop"), None)
    return jax.shard_map(
        shards,
        mesh=mesh,
        in_specs=(placed,) * 4,
        out_specs=placed,
        check_vma=False,
    )
```

time: 168 us -> 99.4 us (0.59)
  waiting for transfers between devices: 68.8 us -> 27.6 us
  matrix products: 36.8 us -> 0 us
  Pallas kernels: 0 us -> 32.3 us
  starting transfers between devices: 4.18 us -> 35 us
  blocking collectives: 19.8 us -> 0 us
  other arithmetic: 18.9 us -> 0.07 us
  between operations: 13.4 us -> 0.17 us
  local copies, waits for them, and re-layouts: 6.05 us -> 3.89 us
    all_gather x2 -> x0, waiting for transfers between devices: 52.7 us -> none  [the longest x1 31.2 us: shards(): lax.all_gather(item_keys, ('row', 'loop'), axis=0, tiled=True)]
    dot_general x2 -> x0, matrix products: 36.8 us -> none  [the longest x1 19 us: make_fold(): lax.dot_general(block_query, key_piece, (((1,), (1,)), ((), ())), preferr...]
    ppermute x0 -> x23, starting transfers between devices: none -> 35 us  [the longest x8 12.3 us: second_hop(): return lax.ppermute(a, PLANE, hops(False, step))]
    pallas_call x0 -> x10, Pallas kernels: none -> 32.3 us  [the longest x6 25.1 us: fold(): pl.pallas_call(kernel, out_shape=out_shape, in_specs=[VMEM] * len(args),...]
    ppermute x0 -> x23, waiting for transfers between devices: none -> 27.6 us  [the longest x4 15.5 us: plane_hop(): return lax.ppermute(a, ('cat',) + PLANE, pairs)]
    all_to_all x1 -> x0, blocking collectives: 19.8 us -> none  [shards(): lax.all_to_all(outgoing.reshape(groups, CAP, feat_width), 'cat', split_ax...]
    reduce_sum x2 -> x0, other arithmetic: 14.8 us -> none  [the longest x1 14.1 us: make_fold(): running_sum = jnp.sum(expo, axis=1)]
    all_to_all x1 -> x0, waiting for transfers between devices: 14.7 us -> none  [shards(): lax.all_to_all(normed.reshape(groups, CAP, feat_width), 'cat', split_axis...]
  transfers between devices with their start and end apart: 3 -> 23, of which waited for: 3 -> 8; matrix products, arithmetic and copies ran while one was open for 24% -> 2% of each run, Pallas kernels for 0% -> 24%
where the time goes in v1:
time: 99.4 us; the launch traced here: 99.1 us
  starting transfers between devices  35 us (35%)
  Pallas kernels  32.3 us (32%)
  waiting for transfers between devices  27.6 us (28%)
  local copies, waits for them, and re-layouts  3.89 us (4%)
    pallas_call x6, Pallas kernels, fold(): pl.pallas_call(kernel, out_shape=out_shape, in_specs=[VMEM] * len(args),...  25.1 us
    ppermute x4, waiting for transfers between devices, plane_hop(): return lax.ppermute(a, ('cat',) + PLANE, pairs)  15.5 us
    ppermute x8, starting transfers between devices, second_hop(): return lax.ppermute(a, PLANE, hops(False, step))  12.3 us
    ppermute x7, starting transfers between devices, swap_cores(): return lax.ppermute(a, PLANE, [(i, i ^ 1) for i in range(32)])  9.18 us
    ppermute x3, waiting for transfers between devices, first_hop(): return lax.ppermute(a, PLANE, hops(True, step))  9.06 us
    ppermute x4, starting transfers between devices, plane_hop(): return lax.ppermute(a, ('cat',) + PLANE, pairs)  8.5 us
    ppermute x3, starting transfers between devices, first_hop(): return lax.ppermute(a, PLANE, hops(True, step))  4.18 us
    unnamed x6, local copies, waits for them, and re-layouts  3.69 us
  transfers between devices with their start and end apart: 23, of which 8 were waited for; matrix products, arithmetic and copies ran while one was open for 2% of the time, Pallas kernels for 24%

profile of v1, /device:TPU:1, one launch (start us, length us, event | category | flops | bytes accessed | tf_op | source)
XLA Modules:
  0.0 99.1 jit_solution(2717804669553727972)
XLA Ops:
  1.4 1.7 %collective-permute-done.far_cat_ref = s32[1,512]{1,0:T(1,128)S(1)} collective-permute-done((s32[1,512]{1,0:T(1,128)}, s32[1,512]{1,0:T(1,128)S(1)}, u32[]{:S(2)}, u32[]{:S(2)}) %collective-permute-start) | collective-permute-done | bytes 2080 | tf_op jit(solution)/shard_map/ppermute | solution.py:46
  6.0 3.9 %collective-permute-start.2 = (bf16[768,512]{1,0:T(8,128)(2,1)S(1)}, bf16[768,512]{1,0:T(8,128)(2,1)S(1)}, u32[]{:S(2)}, u32[]{:S(2)}) collective-permute-start(bf16[768,512]{1,0:T(8,128)(2,1)S(1)} %get-tuple-element.41), channel_id=1, source_target_pairs={{0,32},{1,97},{2,34},{3,99},{4,36},{5,101},{6,38},{7,103},{8,40},{... | collective-permute-start | bytes 2359304 | tf_op jit(solution)/shard_map/ppermute | solution.py:55
  13.2 1.5 %collective-permute-start.4 = (bf16[512,512]{1,0:T(8,128)(2,1)S(1)}, bf16[512,512]{1,0:T(8,128)(2,1)S(1)}, u32[]{:S(2)}, u32[]{:S(2)}) collective-permute-start(bf16[512,512]{1,0:T(8,128)(2,1)S(1)} %get-tuple-element.74.refs_0_), channel_id=1, source_target_pairs={{0,24},{1,7},{2,26},{3,1},{4,28},{5,3},{6,30},{7,5},{8,0},{9,15},{... | collective-permute-start | bytes 1572872 | tf_op jit(solution)/shard_map/ppermute | solution.py:38
  14.7 6.5 %collective-permute-done.3.refs_1_ = bf16[512,512]{1,0:T(8,128)(2,1)S(1)} collective-permute-done((bf16[512,512]{1,0:T(8,128)(2,1)S(1)}, bf16[512,512]{1,0:T(8,128)(2,1)S(1)}, u32[]{:S(2)}, u32[]{:S(2)}) %collective-permute-start.3) | collective-permute-done | bytes 524320 | tf_op jit(solution)/shard_map/ppermute | solution.py:38
  22.6 2.6 %collective-permute-start.17 = (bf16[1024,512]{1,0:T(8,128)(2,1)S(1)}, bf16[1024,512]{1,0:T(8,128)(2,1)S(1)}, u32[]{:S(2)}, u32[]{:S(2)}) collective-permute-start(bf16[1024,512]{1,0:T(8,128)(2,1)S(1)} %pad_maximum_fusion), channel_id=1, source_target_pairs={{0,6},{1,25},{2,0},{3,27},{4,2},{5,29},{6,4},{7,31},{8,14},{9,1},{... | collective-permute-start | bytes 3145736 | tf_op jit(solution)/shard_map/ppermute | solution.py:42
  25.3 3.1 %shard_map.47 = (f32[1024,512]{1,0:T(8,128)S(1)}, f32[1024,128]{1,0:T(8,128)S(1)}, f32[1024,512]{1,0:T(8,128)S(1)}, f32[1024,128]{1,0:T(8,128)S(1)}) custom-call(bf16[512,512]{1,0:T(8,128)(2,1)S(1)} %get-tuple-element.74.refs_0_, bf16[512,512]{1,0:T(8,128)(2,1)S(1)} %collective-permute-done.3.refs_1_, bf16[512,512]{1,0:T(8,128)(2,1)S(1)} %collective-permute-done.4.refs_2_, ...), custom_call_target="tpu_custom_call" | custom-call | flops 2415919104 | bytes 393216 | tf_op jit(solution)/shard_map/pallas_call | solution.py:207
  28.3 2.5 %collective-permute-done.7.refs_3_ = bf16[512,512]{1,0:T(8,128)(2,1)S(1)} collective-permute-done((bf16[512,512]{1,0:T(8,128)(2,1)S(1)}, bf16[512,512]{1,0:T(8,128)(2,1)S(1)}, u32[]{:S(2)}, u32[]{:S(2)}) %collective-permute-start.7) | collective-permute-done | bytes 524320 | tf_op jit(solution)/shard_map/ppermute | solution.py:38
  30.9 3.7 %collective-permute-start.10 = (bf16[1024,512]{1,0:T(8,128)(2,1)S(1)}, bf16[1024,512]{1,0:T(8,128)(2,1)S(1)}, u32[]{:S(2)}, u32[]{:S(2)}) collective-permute-start(bf16[1024,512]{1,0:T(8,128)(2,1)S(1)} %constant_dynamic-update-slice_fusion.2), channel_id=1, source_target_pairs={{0,6},{1,25},{2,0},{3,27},{4,2},{5,29},{6,4},{7,31},{8,14},{9,1},{... | collective-permute-start | bytes 3145736 | tf_op jit(solution)/shard_map/ppermute | solution.py:42
  34.6 2.6 %collective-permute-start.6 = (bf16[256,512]{1,0:T(8,128)(2,1)S(1)}, bf16[256,512]{1,0:T(8,128)(2,1)S(1)}, u32[]{:S(2)}, u32[]{:S(2)}) collective-permute-start(bf16[256,512]{1,0:T(8,128)(2,1)S(1)} %slice.15), channel_id=1, source_target_pairs={{0,32},{1,97},{2,34},{3,99},{4,36},{5,101},{6,38},{7,103},{8,40},{... | collective-permute-start | bytes 786440 | tf_op jit(solution)/shard_map/ppermute | solution.py:55
  37.2 3.8 %collective-permute-done.6.refs_8_.refs_6_.refs_3_ = bf16[256,512]{1,0:T(8,128)(2,1)S(1)} collective-permute-done((bf16[256,512]{1,0:T(8,128)(2,1)S(1)}, bf16[256,512]{1,0:T(8,128)(2,1)S(1)}, u32[]{:S(2)}, u32[]{:S(2)}) %collective-permute-start.6) | collective-permute-done | bytes 262176 | tf_op jit(solution)/shard_map/ppermute | solution.py:55
  41.0 5.8 %collective-permute-start.15 = (bf16[256,512]{1,0:T(8,128)(2,1)S(1)}, bf16[256,512]{1,0:T(8,128)(2,1)S(1)}, u32[]{:S(2)}, u32[]{:S(2)}) collective-permute-start(bf16[256,512]{1,0:T(8,128)(2,1)S(1)} %collective-permute-done.6.refs_8_.refs_6_.refs_3_), channel_id=1, source_target_pairs={{0,1},{1,0},{2,3},{3,2},{4,5},{5,4},{6,7},{7,6},{8,9},{9,8},{10,11... | collective-permute-start | bytes 786440 | tf_op jit(solution)/shard_map/ppermute | solution.py:46
  47.9 4.3 %shard_map.48 = (f32[1024,512]{1,0:T(8,128)S(1)}, f32[1024,128]{1,0:T(8,128)S(1)}, f32[1024,512]{1,0:T(8,128)S(1)}, f32[1024,128]{1,0:T(8,128)S(1)}) custom-call(bf16[512,512]{1,0:T(8,128)(2,1)S(1)} %get-tuple-element.74.refs_0_, ...), custom_call_target="tpu_custom_call", output_to_operand_aliasing={{0}: (10, {}), {1}: (11, {}), {2}: (12, {}), {3}: (13, {})} | custom-call | flops 1879048192 | bytes 524288 | tf_op jit(solution)/shard_map/pallas_call | solution.py:207
  52.2 3.1 %collective-permute-start.18 = (bf16[512,512]{1,0:T(8,128)(2,1)S(1)}, bf16[512,512]{1,0:T(8,128)(2,1)S(1)}, u32[]{:S(2)}, u32[]{:S(2)}) collective-permute-start(bf16[512,512]{1,0:T(8,128)(2,1)S(1)} %slice.23), channel_id=1, source_target_pairs={{0,6},{1,25},{2,0},{3,27},{4,2},{5,29},{6,4},{7,31},{8,14},{9,1},{... | collective-permute-start | bytes 1572872 | tf_op jit(solution)/shard_map/ppermute | solution.py:42
  55.4 2.7 %collective-permute-start.11 = (bf16[512,512]{1,0:T(8,128)(2,1)S(1)}, bf16[512,512]{1,0:T(8,128)(2,1)S(1)}, u32[]{:S(2)}, u32[]{:S(2)}) collective-permute-start(bf16[512,512]{1,0:T(8,128)(2,1)S(1)} %slice.21), channel_id=1, source_target_pairs={{0,6},{1,25},{2,0},{3,27},{4,2},{5,29},{6,4},{7,31},{8,14},{9,1},{... | collective-permute-start | bytes 1572872 | tf_op jit(solution)/shard_map/ppermute | solution.py:42
  58.3 6.0 %shard_map.49 = (f32[1024,512]{1,0:T(8,128)S(1)}, f32[1024,128]{1,0:T(8,128)S(1)}, f32[1024,512]{1,0:T(8,128)S(1)}, f32[1024,128]{1,0:T(8,128)S(1)}) custom-call(bf16[1024,512]{1,0:T(8,128)(2,1)S(1)} %collective-permute-done.14.refs_0_, ...), custom_call_target="tpu_custom_call", output_to_operand_aliasing={{0}: (8, {}), {1}: (9, {}), {2}: (10, {}), {3}: (11, {})} | custom-call | flops 4294967296 | bytes 262144 | tf_op jit(solution)/shard_map/pallas_call | solution.py:207
  64.3 6.0 %shard_map.50 = (f32[1024,512]{1,0:T(8,128)S(1)}, f32[1024,128]{1,0:T(8,128)S(1)}, f32[1024,512]{1,0:T(8,128)S(1)}, f32[1024,128]{1,0:T(8,128)S(1)}) custom-call(bf16[1024,512]{1,0:T(8,128)(2,1)S(1)} %collective-permute-done.8.refs_0_, ...), custom_call_target="tpu_custom_call", output_to_operand_aliasing={{0}: (8, {}), {1}: (9, {}), {2}: (10, {}), {3}: (11, {})} | custom-call | flops 4294967296 | bytes 262144 | tf_op jit(solution)/shard_map/pallas_call | solution.py:207
  70.5 3.3 %shard_map.52 = bf16[1024,640]{1,0:T(8,128)(2,1)S(1)} custom-call(bf16[512,512]{1,0:T(8,128)(2,1)S(1)} %collective-permute-done.16.refs_0_, bf16[512,512]{1,0:T(8,128)(2,1)S(1)} %collective-permute-done.18.refs_1_, bf16[256,512]{1,0:T(8,128)(2,1)S(1)} %get-tuple-element.40.refs_3_.refs_4_.refs_2_.refs_0_, ...), custom_call_target="tpu_custom_call" | custom-call | flops 1073741824 | bytes 262144 | tf_op jit(solution)/shard_map/pallas_call | solution.py:207
  73.8 1.5 %collective-permute-start.19 = (bf16[1024,640]{1,0:T(8,128)(2,1)S(1)}, bf16[1024,640]{1,0:T(8,128)(2,1)S(1)}, u32[]{:S(2)}, u32[]{:S(2)}) collective-permute-start(bf16[1024,640]{1,0:T(8,128)(2,1)S(1)} %shard_map.52), channel_id=1, source_target_pairs={{0,1},{1,0},{2,3},{3,2},{4,5},{5,4},{6,7},{7,6},{8,9},{9,8},{10,11... | collective-permute-start | bytes 3932168 | tf_op jit(solution)/shard_map/ppermute | solution.py:46
  75.8 2.5 %shard_map.51 = (f32[1024,512]{1,0:T(8,128)S(1)}, f32[1024,128]{1,0:T(8,128)S(1)}) custom-call(bf16[512,512]{1,0:T(8,128)(2,1)S(1)} %collective-permute-done.16.refs_0_, bf16[512,512]{1,0:T(8,128)(2,1)S(1)} %collective-permute-done.18.refs_1_, ...), custom_call_target="tpu_custom_call", output_to_operand_aliasing={{0}: (8, {}), {1}: (9, {})} | custom-call | flops 1073741824 | bytes 262144 | tf_op jit(solution)/shard_map/pallas_call | solution.py:207
  78.3 1.6 %shard_map.53 = (f32[1024,512]{1,0:T(8,128)S(1)}, f32[1024,128]{1,0:T(8,128)S(1)}) custom-call(f32[1024,512]{1,0:T(8,128)S(1)} %get-tuple-element.63.acc, f32[1024,128]{1,0:T(8,128)S(1)} %get-tuple-element.64.ml, bf16[1024,640]{1,0:T(8,128)(2,1)S(1)} %collective-permute-done.19.other), custom_call_target="tpu_custom_call", output_to_operand_aliasing={{0}: (0, {}), {1}: (1, {})} | custom-call | tf_op jit(solution)/shard_map/pallas_call | solution.py:236
  79.9 3.0 %shard_map.54 = (bf16[256,512]{1,0:T(8,128)(2,1)S(1)}, bf16[256,512]{1,0:T(8,128)(2,1)S(1)}, bf16[256,512]{1,0:T(8,128)(2,1)S(1)}, bf16[256,512]{1,0:T(8,128)(2,1)S(1)}) custom-call(bf16[256,512]{1,0:T(8,128)(2,1)S(1)} %get-tuple-element.40.refs_3_.refs_4_.refs_2_.refs_0_, bf16[768,512]{1,0:T(8,128)(2,1)S(1)} %collective-permute-done.2.refs_4_.refs_5_.refs_3_.refs_1_, ...), custom_call_target="tpu_custom_call" | custom-call | tf_op jit(solution)/shard_map/pallas_call | solution.py:268
  83.9 2.0 %collective-permute-start.22 = (bf16[256,512]{1,0:T(8,128)(2,1)S(1)}, bf16[256,512]{1,0:T(8,128)(2,1)S(1)}, u32[]{:S(2)}, u32[]{:S(2)}) collective-permute-start(bf16[256,512]{1,0:T(8,128)(2,1)S(1)} %get-tuple-element.72), channel_id=1, source_target_pairs={{0,32},{1,97},{2,34},{3,99},{4,36},{5,101},{6,38},{7,103},{8,40},{... | collective-permute-start | bytes 786440 | tf_op jit(solution)/shard_map/ppermute | solution.py:55
  85.9 11.1 %collective-permute-done.20.r1 = bf16[256,512]{1,0:T(8,128)(2,1)S(1)} collective-permute-done((bf16[256,512]{1,0:T(8,128)(2,1)S(1)}, bf16[256,512]{1,0:T(8,128)(2,1)S(1)}, u32[]{:S(2)}, u32[]{:S(2)}) %collective-permute-start.20) | collective-permute-done | bytes 262176 | tf_op jit(solution)/shard_map/ppermute | solution.py:55
  97.6 1.5 %shard_map.55 = bf16[512,512]{1,0:T(8,128)(2,1)} custom-call(s32[512,128]{1,0:T(8,128)S(1)} %get-tuple-element.39.slot_ref, bf16[256,512]{1,0:T(8,128)(2,1)S(1)} %get-tuple-element.69.r0, bf16[256,512]{1,0:T(8,128)(2,1)S(1)} %collective-permute-done.20.r1, bf16[256,512]{1,0:T(8,128)(2,1)S(1)} %collective-permute-done.21.r2, ...), custom_call_target="tpu_custom_call" | custom-call | tf_op jit(solution)/shard_map/pallas_call | solution.py:291
  (45 shorter events, 12.5 us)
Async XLA Ops:
  0.0 3.2 %collective-permute-start.1 = (bf16[512,512]{1,0:T(8,128)(2,1)}, bf16[512,512]{1,0:T(8,128)(2,1)S(1)}, u32[]{:S(2)}, u32[]{:S(2)}) collective-permute-start(bf16[512,512]{1,0:T(8,128)(2,1)} %q_ref.1), channel_id=1, source_target_pairs={{0,1},{1,0},{2,3},{3,2},{4,5},{5,4},{6,7},{7,6},{8,9},{9,8},{10,11... | collective-permute-start | bytes 1572872 | tf_op jit(solution)/shard_map/ppermute | solution.py:46
  1.4 1.8 %collective-permute-start = (s32[1,512]{1,0:T(1,128)}, s32[1,512]{1,0:T(1,128)S(1)}, u32[]{:S(2)}, u32[]{:S(2)}) collective-permute-start(s32[1,512]{1,0:T(1,128)} %bitcast.1), channel_id=1, source_target_pairs={{0,1},{1,0},{2,3},{3,2},{4,5},{5,4},{6,7},{7,6},{8,9},{9,8},{10,11... | collective-permute-start | bytes 6152 | tf_op jit(solution)/shard_map/ppermute | solution.py:46
  3.2 1.0 %copy-start = (bf16[512,512]{1,0:T(8,128)(2,1)S(1)}, bf16[512,512]{1,0:T(8,128)(2,1)}, u32[]{:S(2)}) copy-start(bf16[512,512]{1,0:T(8,128)(2,1)} %q_ref.1) | copy-start | bytes 1572868
  6.0 15.3 %collective-permute-start.2 = (bf16[768,512]{1,0:T(8,128)(2,1)S(1)}, bf16[768,512]{1,0:T(8,128)(2,1)S(1)}, u32[]{:S(2)}, u32[]{:S(2)}) collective-permute-start(bf16[768,512]{1,0:T(8,128)(2,1)S(1)} %get-tuple-element.41), channel_id=1, source_target_pairs={{0,32},{1,97},{2,34},{3,99},{4,36},{5,101},{6,38},{7,103},{8,40},{... | collective-permute-start | bytes 2359304 | tf_op jit(solution)/shard_map/ppermute | solution.py:55
  11.9 9.4 %collective-permute-start.3 = (bf16[512,512]{1,0:T(8,128)(2,1)S(1)}, bf16[512,512]{1,0:T(8,128)(2,1)S(1)}, u32[]{:S(2)}, u32[]{:S(2)}) collective-permute-start(bf16[512,512]{1,0:T(8,128)(2,1)S(1)} %get-tuple-element.74.refs_0_), channel_id=1, source_target_pairs={{0,8},{1,3},{2,10},{3,5},{4,12},{5,7},{6,14},{7,1},{8,16},{9,11},{... | collective-permute-start | bytes 1572872 | tf_op jit(solution)/shard_map/ppermute | solution.py:38
  13.2 8.0 %collective-permute-start.4 = (bf16[512,512]{1,0:T(8,128)(2,1)S(1)}, bf16[512,512]{1,0:T(8,128)(2,1)S(1)}, u32[]{:S(2)}, u32[]{:S(2)}) collective-permute-start(bf16[512,512]{1,0:T(8,128)(2,1)S(1)} %get-tuple-element.74.refs_0_), channel_id=1, source_target_pairs={{0,24},{1,7},{2,26},{3,1},{4,28},{5,3},{6,30},{7,5},{8,0},{9,15},{... | collective-permute-start | bytes 1572872 | tf_op jit(solution)/shard_map/ppermute | solution.py:38
  21.3 4.0 %collective-permute-start.5 = (bf16[768,512]{1,0:T(8,128)(2,1)S(1)}, bf16[768,512]{1,0:T(8,128)(2,1)S(1)}, u32[]{:S(2)}, u32[]{:S(2)}) collective-permute-start(bf16[768,512]{1,0:T(8,128)(2,1)S(1)} %collective-permute-done.2.refs_4_.refs_5_.refs_3_.refs_1_), channel_id=1, source_target_pairs={{0,1},{1,0},{2,3},{3,2},{4,5},{5,4},{6,7},{7,6},{8,9},{9,8},{10,11... | collective-permute-start | bytes 2359304 | tf_op jit(solution)/shard_map/ppermute | solution.py:46
  21.3 9.6 %collective-permute-start.7 = (bf16[512,512]{1,0:T(8,128)(2,1)S(1)}, bf16[512,512]{1,0:T(8,128)(2,1)S(1)}, u32[]{:S(2)}, u32[]{:S(2)}) collective-permute-start(bf16[512,512]{1,0:T(8,128)(2,1)S(1)} %collective-permute-done.3.refs_1_), channel_id=1, source_target_pairs={{0,8},{1,3},{2,10},{3,5},{4,12},{5,7},{6,14},{7,1},{8,16},{9,11},{... | collective-permute-start | bytes 1572872 | tf_op jit(solution)/shard_map/ppermute | solution.py:38
  22.6 24.1 %collective-permute-start.17 = (bf16[1024,512]{1,0:T(8,128)(2,1)S(1)}, bf16[1024,512]{1,0:T(8,128)(2,1)S(1)}, u32[]{:S(2)}, u32[]{:S(2)}) collective-permute-start(bf16[1024,512]{1,0:T(8,128)(2,1)S(1)} %pad_maximum_fusion), channel_id=1, source_target_pairs={{0,6},{1,25},{2,0},{3,27},{4,2},{5,29},{6,4},{7,31},{8,14},{9,1},{... | collective-permute-start | bytes 3145736 | tf_op jit(solution)/shard_map/ppermute | solution.py:42
  25.2 21.6 %collective-permute-start.14 = (bf16[1024,512]{1,0:T(8,128)(2,1)S(1)}, bf16[1024,512]{1,0:T(8,128)(2,1)S(1)}, u32[]{:S(2)}, u32[]{:S(2)}) collective-permute-start(bf16[1024,512]{1,0:T(8,128)(2,1)S(1)} %pad_maximum_fusion), channel_id=1, source_target_pairs={{0,2},{1,9},{2,4},{3,11},{4,6},{5,13},{6,0},{7,15},{8,10},{9,17},{... | collective-permute-start | bytes 3145736 | tf_op jit(solution)/shard_map/ppermute | solution.py:42
  30.9 24.5 %collective-permute-start.10 = (bf16[1024,512]{1,0:T(8,128)(2,1)S(1)}, bf16[1024,512]{1,0:T(8,128)(2,1)S(1)}, u32[]{:S(2)}, u32[]{:S(2)}) collective-permute-start(bf16[1024,512]{1,0:T(8,128)(2,1)S(1)} %constant_dynamic-update-slice_fusion.2), channel_id=1, source_target_pairs={{0,6},{1,25},{2,0},{3,27},{4,2},{5,29},{6,4},{7,31},{8,14},{9,1},{... | collective-permute-start | bytes 3145736 | tf_op jit(solution)/shard_map/ppermute | solution.py:42
  34.6 23.6 %collective-permute-start.8 = (bf16[1024,512]{1,0:T(8,128)(2,1)S(1)}, bf16[1024,512]{1,0:T(8,128)(2,1)S(1)}, u32[]{:S(2)}, u32[]{:S(2)}) collective-permute-start(bf16[1024,512]{1,0:T(8,128)(2,1)S(1)} %constant_dynamic-update-slice_fusion.2), channel_id=1, source_target_pairs={{0,2},{1,9},{2,4},{3,11},{4,6},{5,13},{6,0},{7,15},{8,10},{9,17},{... | collective-permute-start | bytes 3145736 | tf_op jit(solution)/shard_map/ppermute | solution.py:42
  34.6 6.4 %collective-permute-start.6 = (bf16[256,512]{1,0:T(8,128)(2,1)S(1)}, bf16[256,512]{1,0:T(8,128)(2,1)S(1)}, u32[]{:S(2)}, u32[]{:S(2)}) collective-permute-start(bf16[256,512]{1,0:T(8,128)(2,1)S(1)} %slice.15), channel_id=1, source_target_pairs={{0,32},{1,97},{2,34},{3,99},{4,36},{5,101},{6,38},{7,103},{8,40},{... | collective-permute-start | bytes 786440 | tf_op jit(solution)/shard_map/ppermute | solution.py:55
  41.0 6.9 %collective-permute-start.15 = (bf16[256,512]{1,0:T(8,128)(2,1)S(1)}, bf16[256,512]{1,0:T(8,128)(2,1)S(1)}, u32[]{:S(2)}, u32[]{:S(2)}) collective-permute-start(bf16[256,512]{1,0:T(8,128)(2,1)S(1)} %collective-permute-done.6.refs_8_.refs_6_.refs_3_), channel_id=1, source_target_pairs={{0,1},{1,0},{2,3},{3,2},{4,5},{5,4},{6,7},{7,6},{8,9},{9,8},{10,11... | collective-permute-start | bytes 786440 | tf_op jit(solution)/shard_map/ppermute | solution.py:46
  52.2 18.3 %collective-permute-start.18 = (bf16[512,512]{1,0:T(8,128)(2,1)S(1)}, bf16[512,512]{1,0:T(8,128)(2,1)S(1)}, u32[]{:S(2)}, u32[]{:S(2)}) collective-permute-start(bf16[512,512]{1,0:T(8,128)(2,1)S(1)} %slice.23), channel_id=1, source_target_pairs={{0,6},{1,25},{2,0},{3,27},{4,2},{5,29},{6,4},{7,31},{8,14},{9,1},{... | collective-permute-start | bytes 1572872 | tf_op jit(solution)/shard_map/ppermute | solution.py:42
  55.4 14.9 %collective-permute-start.16 = (bf16[512,512]{1,0:T(8,128)(2,1)S(1)}, bf16[512,512]{1,0:T(8,128)(2,1)S(1)}, u32[]{:S(2)}, u32[]{:S(2)}) collective-permute-start(bf16[512,512]{1,0:T(8,128)(2,1)S(1)} %slice.22), channel_id=1, source_target_pairs={{0,2},{1,9},{2,4},{3,11},{4,6},{5,13},{6,0},{7,15},{8,10},{9,17},{... | collective-permute-start | bytes 1572872 | tf_op jit(solution)/shard_map/ppermute | solution.py:42
  55.4 14.9 %collective-permute-start.11 = (bf16[512,512]{1,0:T(8,128)(2,1)S(1)}, bf16[512,512]{1,0:T(8,128)(2,1)S(1)}, u32[]{:S(2)}, u32[]{:S(2)}) collective-permute-start(bf16[512,512]{1,0:T(8,128)(2,1)S(1)} %slice.21), channel_id=1, source_target_pairs={{0,6},{1,25},{2,0},{3,27},{4,2},{5,29},{6,4},{7,31},{8,14},{9,1},{... | collective-permute-start | bytes 1572872 | tf_op jit(solution)/shard_map/ppermute | solution.py:42
  58.2 12.3 %collective-permute-start.9 = (bf16[512,512]{1,0:T(8,128)(2,1)S(1)}, bf16[512,512]{1,0:T(8,128)(2,1)S(1)}, u32[]{:S(2)}, u32[]{:S(2)}) collective-permute-start(bf16[512,512]{1,0:T(8,128)(2,1)S(1)} %slice.20), channel_id=1, source_target_pairs={{0,2},{1,9},{2,4},{3,11},{4,6},{5,13},{6,0},{7,15},{8,10},{9,17},{... | collective-permute-start | bytes 1572872 | tf_op jit(solution)/shard_map/ppermute | solution.py:42
  73.8 4.5 %collective-permute-start.19 = (bf16[1024,640]{1,0:T(8,128)(2,1)S(1)}, bf16[1024,640]{1,0:T(8,128)(2,1)S(1)}, u32[]{:S(2)}, u32[]{:S(2)}) collective-permute-start(bf16[1024,640]{1,0:T(8,128)(2,1)S(1)} %shard_map.52), channel_id=1, source_target_pairs={{0,1},{1,0},{2,3},{3,2},{4,5},{5,4},{6,7},{7,6},{8,9},{9,8},{10,11... | collective-permute-start | bytes 3932168 | tf_op jit(solution)/shard_map/ppermute | solution.py:46
  75.3 4.6 %collective-permute-start.12 = (bf16[512,512]{1,0:T(8,128)(2,1)S(1)}, bf16[512,512]{1,0:T(8,128)(2,1)S(1)}, u32[]{:S(2)}, u32[]{:S(2)}) collective-permute-start(bf16[512,512]{1,0:T(8,128)(2,1)S(1)} %collective-permute-done.9.refs_4_), channel_id=1, source_target_pairs={{0,1},{1,0},{2,3},{3,2},{4,5},{5,4},{6,7},{7,6},{8,9},{9,8},{10,11... | collective-permute-start | bytes 1572872 | tf_op jit(solution)/shard_map/ppermute | solution.py:46
  75.4 4.5 %collective-permute-start.13 = (bf16[512,512]{1,0:T(8,128)(2,1)S(1)}, bf16[512,512]{1,0:T(8,128)(2,1)S(1)}, u32[]{:S(2)}, u32[]{:S(2)}) collective-permute-start(bf16[512,512]{1,0:T(8,128)(2,1)S(1)} %collective-permute-done.11.refs_5_), channel_id=1, source_target_pairs={{0,1},{1,0},{2,3},{3,2},{4,5},{5,4},{6,7},{7,6},{8,9},{9,8},{10,11... | collective-permute-start | bytes 1572872 | tf_op jit(solution)/shard_map/ppermute | solution.py:46
  83.0 14.1 %collective-permute-start.20 = (bf16[256,512]{1,0:T(8,128)(2,1)S(1)}, bf16[256,512]{1,0:T(8,128)(2,1)S(1)}, u32[]{:S(2)}, u32[]{:S(2)}) collective-permute-start(bf16[256,512]{1,0:T(8,128)(2,1)S(1)} %get-tuple-element.70), channel_id=1, source_target_pairs={{0,96},{1,33},{2,98},{3,35},{4,100},{5,37},{6,102},{7,39},{8,104},... | collective-permute-start | bytes 786440 | tf_op jit(solution)/shard_map/ppermute | solution.py:55
  83.0 14.0 %collective-permute-start.21 = (bf16[256,512]{1,0:T(8,128)(2,1)S(1)}, bf16[256,512]{1,0:T(8,128)(2,1)S(1)}, u32[]{:S(2)}, u32[]{:S(2)}) collective-permute-start(bf16[256,512]{1,0:T(8,128)(2,1)S(1)} %get-tuple-element.71), channel_id=1, source_target_pairs={{0,64},{32,96},{64,0},{96,32},{1,65},{33,97},{65,1},{97,33},{2,66}... | collective-permute-start | bytes 786440 | tf_op jit(solution)/shard_map/ppermute | solution.py:59
  83.9 13.6 %collective-permute-start.22 = (bf16[256,512]{1,0:T(8,128)(2,1)S(1)}, bf16[256,512]{1,0:T(8,128)(2,1)S(1)}, u32[]{:S(2)}, u32[]{:S(2)}) collective-permute-start(bf16[256,512]{1,0:T(8,128)(2,1)S(1)} %get-tuple-element.72), channel_id=1, source_target_pairs={{0,32},{1,97},{2,34},{3,99},{4,36},{5,101},{6,38},{7,103},{8,40},{... | collective-permute-start | bytes 786440 | tf_op jit(solution)/shard_map/ppermute | solution.py:55
  (1 other events, 0.7 us)

commit v2 on v1

--- a/solution.py
+++ b/solution.py
@@ -153,8 +153,12 @@
     outs = rest
     jobs = []
     for i, (blocks, begin) in enumerate(plan):
+        group, rows = i // CATS, pl.ds(i % CATS * CAP, CAP)
         if blocks:
-            jobs.append((i // CATS, i % CATS, tiles[i], blocks, begin))
+            jobs.append((group, i % CATS, tiles[i], blocks, begin))
+        elif not begin:
+            for ref, out in zip(states[group], outs[2 * group : 2 * group + 2]):
+                out[rows, :] = ref[rows, :]
 
     def score(job):
         ref, row = job[2]
@@ -300,12 +304,14 @@
 def shards(queries, categories, item_keys, item_values):
     rows = queries.shape[0]
     cats = categories.reshape(1, rows)
-    q0, sent, far_q0, slots = dispatch(cats, swap_cores(cats), queries, swap_cores(queries))
     here = jnp.concatenate([item_keys, item_values], axis=0)
+    far_cats = after(swap_cores(cats), here)
+    q0, sent, far_q0, slots = dispatch(cats, far_cats, queries, swap_cores(queries))
     left, right = first_hop(here, 1), first_hop(here, -1)
     q12 = after(plane_hop(sent, 1), left, right)
     q2 = plane_hop(q12[2 * CAP :], 1)
-    far_q12, far_q2 = swap_cores(q12), swap_cores(q2)
+    far_q12 = swap_cores(q12)
+    far_q2 = swap_cores(after(q2, far_q12))
     early = [q0, q12, far_q0, far_q12]
     qs = early + [q2, far_q2]
     own = ((0, 0), (1, 0), (3, CAP), (4, 0))
@@ -323,23 +329,26 @@
 
     first = tuple(whole(i) for i in range(3))
     plan = (((first, True),) * 3 + (((), True),)) * 2
-    state = fold(early, tiles, [here, left, right], plan, None, weight=1)
+    state = fold(early, tiles, [here, left, right], plan, None, weight=0.3)
     rest = jnp.concatenate([here, after(far, state[0][1])], axis=0)
     up_rest, down_rest = second_hop(rest, 1), second_hop(rest, -1)
     own_far = whole(3)
     plan = ((((own_far,), False),) * 3 + ((first + (own_far,), True),)) * 2
     state = fold(qs, tiles, [here, left, right, far], plan, state, weight=1)
-    up_left = second_hop(after(up_pair[:two], state[0][1]), 1)
-    down_right = second_hop(after(down_pair[two:], state[0][1]), -1)
+    up_pair, down_pair = after(up_pair, state[0][1]), after(down_pair, state[0][1])
+    up_left, down_right = second_hop(up_pair[:two], 1), second_hop(down_pair[two:], -1)
     both = same([whole(i, j) for i in range(2) for j in (0, two)])
     state = fold(qs, tiles, [up_pair, down_pair], both, state, weight=1)
     up_here = second_hop(up_rest[:two], 1)
     down_far = second_hop(down_rest[two:], -1)
-    mine, others = fold(qs, tiles, [up_rest, down_rest], both, state, weight=1)
-    tail = [after(up_left, up_here, down_far), down_right]
-    last_plan = same([whole(0), whole(1)])[:CATS]
-    other = swap_cores(fold(qs, theirs, tail, last_plan, [others], True, weight=1))
-    (mine,) = fold(qs, own, tail, last_plan, [mine], weight=1)
+    mine, others = state
+    tail = [up_rest, down_rest, up_left, down_right]
+    blocks = tuple([whole(i, j) for i in range(2) for j in (0, two)] + [whole(2), whole(3)])
+    todo, skip = (blocks, False), ((), False)
+    other = swap_cores(fold(qs, theirs, tail, (todo,) * 4, [others], True, weight=3))
+    (mine,) = fold(qs, own, tail, (todo, todo, skip, skip), [mine], weight=3)
+    tail = [after(up_rest, up_here, down_far), down_rest, up_left, down_right]
+    (mine,) = fold(qs, own, tail, (skip, skip, todo, todo), [mine], weight=3)
     merged = merge(mine, other)
     last = [up_here, down_far]
     last += [swap_cores(a) for a in last]

time: 99.4 us -> 94 us (0.946)
  Pallas kernels: 32.3 us -> 29.8 us
  waiting for transfers between devices: 27.6 us -> 25.3 us
    ppermute x4, waiting for transfers between devices: 15.5 us -> 5.13 us  [plane_hop(): return lax.ppermute(a, ('cat',) + PLANE, pairs)]
    ppermute x1, waiting for transfers between devices: 0.01 us -> 6.02 us  [opposite_plane(): return lax.ppermute(a, 'cat', [(i, (i + 2) % CATS) for i in range(CATS)])]
    ppermute x8, waiting for transfers between devices: 0.26 us -> 4.77 us  [second_hop(): return lax.ppermute(a, PLANE, hops(False, step))]
    pallas_call x6, Pallas kernels: 25.1 us -> 22.6 us  [fold(): pl.pallas_call(kernel, out_shape=out_shape, in_specs=[VMEM] * len(args),...]
    ppermute x1, starting transfers between devices: 0.91 us -> 3.02 us  [opposite_plane(): return lax.ppermute(a, 'cat', [(i, (i + 2) % CATS) for i in range(CATS)])]
    ppermute x4, starting transfers between devices: 8.5 us -> 6.51 us  [plane_hop(): return lax.ppermute(a, ('cat',) + PLANE, pairs)]
    ppermute x7, waiting for transfers between devices: 2.83 us -> 1.18 us  [swap_cores(): return lax.ppermute(a, PLANE, [(i, i ^ 1) for i in range(32)])]
    ppermute x7, starting transfers between devices: 9.18 us -> 8.06 us  [swap_cores(): return lax.ppermute(a, PLANE, [(i, i ^ 1) for i in range(32)])]
  transfers between devices with their start and end apart: 23 -> 23, of which waited for: 8 -> 8; matrix products, arithmetic and copies ran while one was open for 2% -> 2% of each run, Pallas kernels for 24% -> 26%
where the time goes in v2:
time: 94 us; the launch traced here: 93.3 us
  starting transfers between devices  34.2 us (36%)
  Pallas kernels  29.8 us (32%)
  waiting for transfers between devices  25.3 us (27%)
  local copies, waits for them, and re-layouts  3.88 us (4%)
    pallas_call x6, Pallas kernels, fold(): pl.pallas_call(kernel, out_shape=out_shape, in_specs=[VMEM] * len(args),...  22.6 us
    ppermute x8, starting transfers between devices, second_hop(): return lax.ppermute(a, PLANE, hops(False, step))  12.5 us
    ppermute x3, waiting for transfers between devices, first_hop(): return lax.ppermute(a, PLANE, hops(True, step))  8.17 us
    ppermute x7, starting transfers between devices, swap_cores(): return lax.ppermute(a, PLANE, [(i, i ^ 1) for i in range(32)])  8.06 us
    ppermute x4, starting transfers between devices, plane_hop(): return lax.ppermute(a, ('cat',) + PLANE, pairs)  6.51 us
    ppermute x1, waiting for transfers between devices, opposite_plane(): return lax.ppermute(a, 'cat', [(i, (i + 2) % CATS) for i in range(CATS)])  6.02 us
    ppermute x4, waiting for transfers between devices, plane_hop(): return lax.ppermute(a, ('cat',) + PLANE, pairs)  5.13 us
    ppermute x8, waiting for transfers between devices, second_hop(): return lax.ppermute(a, PLANE, hops(False, step))  4.77 us
  transfers between devices with their start and end apart: 23, of which 8 were waited for; matrix products, arithmetic and copies ran while one was open for 2% of the time, Pallas kernels for 26%

profile of v2, /device:TPU:1, one launch (start us, length us, event | category | flops | bytes accessed | tf_op | source)
XLA Modules:
  0.0 93.3 jit_solution(5095152249053006078)
XLA Ops:
  6.2 3.9 %collective-permute-start.2 = (bf16[768,512]{1,0:T(8,128)(2,1)S(1)}, bf16[768,512]{1,0:T(8,128)(2,1)S(1)}, u32[]{:S(2)}, u32[]{:S(2)}) collective-permute-start(bf16[768,512]{1,0:T(8,128)(2,1)S(1)} %get-tuple-element.42), channel_id=1, source_target_pairs={{0,32},{1,97},{2,34},{3,99},{4,36},{5,101},{6,38},{7,103},{8,40},{... | collective-permute-start | bytes 2359304 | tf_op jit(solution)/shard_map/ppermute | solution.py:55
  12.9 6.9 %collective-permute-done.3.refs_1_ = bf16[512,512]{1,0:T(8,128)(2,1)S(1)} collective-permute-done((bf16[512,512]{1,0:T(8,128)(2,1)S(1)}, bf16[512,512]{1,0:T(8,128)(2,1)S(1)}, u32[]{:S(2)}, u32[]{:S(2)}) %collective-permute-start.3) | collective-permute-done | bytes 524320 | tf_op jit(solution)/shard_map/ppermute | solution.py:38
  22.3 2.5 %collective-permute-start.17 = (bf16[1024,512]{1,0:T(8,128)(2,1)S(1)}, bf16[1024,512]{1,0:T(8,128)(2,1)S(1)}, u32[]{:S(2)}, u32[]{:S(2)}) collective-permute-start(bf16[1024,512]{1,0:T(8,128)(2,1)S(1)} %pad_maximum_fusion), channel_id=1, source_target_pairs={{0,6},{1,25},{2,0},{3,27},{4,2},{5,29},{6,4},{7,31},{8,14},{9,1},{... | collective-permute-start | bytes 3145736 | tf_op jit(solution)/shard_map/ppermute | solution.py:42
  24.8 1.8 %collective-permute-start.6 = (bf16[256,512]{1,0:T(8,128)(2,1)S(1)}, bf16[256,512]{1,0:T(8,128)(2,1)S(1)}, u32[]{:S(2)}, u32[]{:S(2)}) collective-permute-start(bf16[256,512]{1,0:T(8,128)(2,1)S(1)} %slice.15), channel_id=1, source_target_pairs={{0,32},{1,97},{2,34},{3,99},{4,36},{5,101},{6,38},{7,103},{8,40},{... | collective-permute-start | bytes 786440 | tf_op jit(solution)/shard_map/ppermute | solution.py:55
  26.6 3.1 %shard_map.47 = (f32[1024,512]{1,0:T(8,128)S(1)}, f32[1024,128]{1,0:T(8,128)S(1)}, f32[1024,512]{1,0:T(8,128)S(1)}, f32[1024,128]{1,0:T(8,128)S(1)}) custom-call(bf16[512,512]{1,0:T(8,128)(2,1)S(1)} %get-tuple-element.74.refs_0_, bf16[512,512]{1,0:T(8,128)(2,1)S(1)} %collective-permute-done.3.refs_1_, bf16[512,512]{1,0:T(8,128)(2,1)S(1)} %collective-permute-done.4.refs_2_, ...), custom_call_target="tpu_custom_call" | custom-call | flops 724774912 | bytes 393216 | tf_op jit(solution)/shard_map/pallas_call | solution.py:211
  31.0 3.6 %collective-permute-start.10 = (bf16[1024,512]{1,0:T(8,128)(2,1)S(1)}, bf16[1024,512]{1,0:T(8,128)(2,1)S(1)}, u32[]{:S(2)}, u32[]{:S(2)}) collective-permute-start(bf16[1024,512]{1,0:T(8,128)(2,1)S(1)} %constant_dynamic-update-slice_fusion.2), channel_id=1, source_target_pairs={{0,6},{1,25},{2,0},{3,27},{4,2},{5,29},{6,4},{7,31},{8,14},{9,1},{... | collective-permute-start | bytes 3145736 | tf_op jit(solution)/shard_map/ppermute | solution.py:42
  34.6 3.2 %collective-permute-start.15 = (bf16[256,512]{1,0:T(8,128)(2,1)S(1)}, bf16[256,512]{1,0:T(8,128)(2,1)S(1)}, u32[]{:S(2)}, u32[]{:S(2)}) collective-permute-start(bf16[256,512]{1,0:T(8,128)(2,1)S(1)} %collective-permute-done.6.refs_8_.refs_6_.refs_3_), channel_id=1, source_target_pairs={{0,1},{1,0},{2,3},{3,2},{4,5},{5,4},{6,7},{7,6},{8,9},{9,8},{10,11... | collective-permute-start | bytes 786440 | tf_op jit(solution)/shard_map/ppermute | solution.py:46
  39.0 4.3 %shard_map.48 = (f32[1024,512]{1,0:T(8,128)S(1)}, f32[1024,128]{1,0:T(8,128)S(1)}, f32[1024,512]{1,0:T(8,128)S(1)}, f32[1024,128]{1,0:T(8,128)S(1)}) custom-call(bf16[512,512]{1,0:T(8,128)(2,1)S(1)} %get-tuple-element.74.refs_0_, ...), custom_call_target="tpu_custom_call", output_to_operand_aliasing={{0}: (10, {}), {1}: (11, {}), {2}: (12, {}), {3}: (13, {})} | custom-call | flops 1879048192 | bytes 524288 | tf_op jit(solution)/shard_map/pallas_call | solution.py:211
  43.3 3.3 %collective-permute-start.18 = (bf16[512,512]{1,0:T(8,128)(2,1)S(1)}, bf16[512,512]{1,0:T(8,128)(2,1)S(1)}, u32[]{:S(2)}, u32[]{:S(2)}) collective-permute-start(bf16[512,512]{1,0:T(8,128)(2,1)S(1)} %slice.19), channel_id=1, source_target_pairs={{0,6},{1,25},{2,0},{3,27},{4,2},{5,29},{6,4},{7,31},{8,14},{9,1},{... | collective-permute-start | bytes 1572872 | tf_op jit(solution)/shard_map/ppermute | solution.py:42
  46.8 6.0 %shard_map.49 = (f32[1024,512]{1,0:T(8,128)S(1)}, f32[1024,128]{1,0:T(8,128)S(1)}, f32[1024,512]{1,0:T(8,128)S(1)}, f32[1024,128]{1,0:T(8,128)S(1)}) custom-call(bf16[1024,512]{1,0:T(8,128)(2,1)S(1)} %collective-permute-done.14.refs_0_, ...), custom_call_target="tpu_custom_call", output_to_operand_aliasing={{0}: (8, {}), {1}: (9, {}), {2}: (10, {}), {3}: (11, {})} | custom-call | flops 4294967296 | bytes 262144 | tf_op jit(solution)/shard_map/pallas_call | solution.py:211
  52.8 2.7 %collective-permute-start.11 = (bf16[512,512]{1,0:T(8,128)(2,1)S(1)}, bf16[512,512]{1,0:T(8,128)(2,1)S(1)}, u32[]{:S(2)}, u32[]{:S(2)}) collective-permute-start(bf16[512,512]{1,0:T(8,128)(2,1)S(1)} %slice.21), channel_id=1, source_target_pairs={{0,6},{1,25},{2,0},{3,27},{4,2},{5,29},{6,4},{7,31},{8,14},{9,1},{... | collective-permute-start | bytes 1572872 | tf_op jit(solution)/shard_map/ppermute | solution.py:42
  55.9 3.1 %collective-permute-done.16.refs_2_ = bf16[512,512]{1,0:T(8,128)(2,1)S(1)} collective-permute-done((bf16[512,512]{1,0:T(8,128)(2,1)S(1)}, bf16[512,512]{1,0:T(8,128)(2,1)S(1)}, u32[]{:S(2)}, u32[]{:S(2)}) %collective-permute-start.16) | collective-permute-done | bytes 524320 | tf_op jit(solution)/shard_map/ppermute | solution.py:42
  59.0 4.2 %shard_map.52 = bf16[1024,640]{1,0:T(8,128)(2,1)S(1)} custom-call(bf16[1024,512]{1,0:T(8,128)(2,1)S(1)} %collective-permute-done.8.refs_0_, bf16[1024,512]{1,0:T(8,128)(2,1)S(1)} %collective-permute-done.10.refs_1_, bf16[512,512]{1,0:T(8,128)(2,1)S(1)} %collective-permute-done.16.refs_2_, bf16[512,512]{1,0:T(8,128)(2,1)S(1)} %collective-permute-done.18.refs_3_, ...), custom_call_target="tpu_custom_call" | custom-call | flops 9663676416 | bytes 524288 | tf_op jit(solution)/shard_map/pallas_call | solution.py:211
  63.7 1.7 %collective-permute-done.9.refs_4_ = bf16[512,512]{1,0:T(8,128)(2,1)S(1)} collective-permute-done((bf16[512,512]{1,0:T(8,128)(2,1)S(1)}, bf16[512,512]{1,0:T(8,128)(2,1)S(1)}, u32[]{:S(2)}, u32[]{:S(2)}) %collective-permute-start.9) | collective-permute-done | bytes 524320 | tf_op jit(solution)/shard_map/ppermute | solution.py:42
  65.4 1.8 %collective-permute-start.12 = (bf16[512,512]{1,0:T(8,128)(2,1)S(1)}, bf16[512,512]{1,0:T(8,128)(2,1)S(1)}, u32[]{:S(2)}, u32[]{:S(2)}) collective-permute-start(bf16[512,512]{1,0:T(8,128)(2,1)S(1)} %collective-permute-done.9.refs_4_), channel_id=1, source_target_pairs={{0,1},{1,0},{2,3},{3,2},{4,5},{5,4},{6,7},{7,6},{8,9},{9,8},{10,11... | collective-permute-start | bytes 1572872 | tf_op jit(solution)/shard_map/ppermute | solution.py:46
  67.2 2.5 %shard_map.50 = (f32[1024,512]{1,0:T(8,128)S(1)}, f32[1024,128]{1,0:T(8,128)S(1)}) custom-call(bf16[1024,512]{1,0:T(8,128)(2,1)S(1)} %collective-permute-done.8.refs_0_, bf16[1024,512]{1,0:T(8,128)(2,1)S(1)} %collective-permute-done.10.refs_1_, bf16[512,512]{1,0:T(8,128)(2,1)S(1)} %collective-permute-done.16.refs_2_, ...), custom_call_target="tpu_custom_call", output_to_operand_aliasing={{0}: (10, {}), {1}: (11, {})} | custom-call | flops 4831838208 | bytes 524288 | tf_op jit(solution)/shard_map/pallas_call | solution.py:211
  69.7 2.5 %shard_map.51 = (f32[1024,512]{1,0:T(8,128)S(1)}, f32[1024,128]{1,0:T(8,128)S(1)}) custom-call(bf16[1024,512]{1,0:T(8,128)(2,1)S(1)} %collective-permute-done.8.refs_0_, bf16[1024,512]{1,0:T(8,128)(2,1)S(1)} %collective-permute-done.10.refs_1_, bf16[512,512]{1,0:T(8,128)(2,1)S(1)} %collective-permute-done.16.refs_2_, ...), custom_call_target="tpu_custom_call", output_to_operand_aliasing={{0}: (10, {}), {1}: (11, {})} | custom-call | flops 4831838208 | bytes 524288 | tf_op jit(solution)/shard_map/pallas_call | solution.py:211
  72.2 1.6 %shard_map.53 = (f32[1024,512]{1,0:T(8,128)S(1)}, f32[1024,128]{1,0:T(8,128)S(1)}) custom-call(f32[1024,512]{1,0:T(8,128)S(1)} %get-tuple-element.63.acc, f32[1024,128]{1,0:T(8,128)S(1)} %get-tuple-element.64.ml, bf16[1024,640]{1,0:T(8,128)(2,1)S(1)} %collective-permute-done.19.other), custom_call_target="tpu_custom_call", output_to_operand_aliasing={{0}: (0, {}), {1}: (1, {})} | custom-call | tf_op jit(solution)/shard_map/pallas_call | solution.py:240
  73.8 3.0 %shard_map.54 = (bf16[256,512]{1,0:T(8,128)(2,1)S(1)}, bf16[256,512]{1,0:T(8,128)(2,1)S(1)}, bf16[256,512]{1,0:T(8,128)(2,1)S(1)}, bf16[256,512]{1,0:T(8,128)(2,1)S(1)}) custom-call(bf16[256,512]{1,0:T(8,128)(2,1)S(1)} %get-tuple-element.41.refs_3_.refs_4_.refs_2_.refs_0_, bf16[768,512]{1,0:T(8,128)(2,1)S(1)} %collective-permute-done.2.refs_4_.refs_5_.refs_3_.refs_1_, ...), custom_call_target="tpu_custom_call" | custom-call | tf_op jit(solution)/shard_map/pallas_call | solution.py:272
  77.0 3.0 %collective-permute-start.21 = (bf16[256,512]{1,0:T(8,128)(2,1)S(1)}, bf16[256,512]{1,0:T(8,128)(2,1)S(1)}, u32[]{:S(2)}, u32[]{:S(2)}) collective-permute-start(bf16[256,512]{1,0:T(8,128)(2,1)S(1)} %get-tuple-element.71), channel_id=1, source_target_pairs={{0,64},{32,96},{64,0},{96,32},{1,65},{33,97},{65,1},{97,33},{2,66}... | collective-permute-start | bytes 786440 | tf_op jit(solution)/shard_map/ppermute | solution.py:59
  80.7 2.7 %collective-permute-done.20.r1 = bf16[256,512]{1,0:T(8,128)(2,1)S(1)} collective-permute-done((bf16[256,512]{1,0:T(8,128)(2,1)S(1)}, bf16[256,512]{1,0:T(8,128)(2,1)S(1)}, u32[]{:S(2)}, u32[]{:S(2)}) %collective-permute-start.20) | collective-permute-done | bytes 262176 | tf_op jit(solution)/shard_map/ppermute | solution.py:55
  83.4 6.0 %collective-permute-done.21.r2 = bf16[256,512]{1,0:T(8,128)(2,1)S(1)} collective-permute-done((bf16[256,512]{1,0:T(8,128)(2,1)S(1)}, bf16[256,512]{1,0:T(8,128)(2,1)S(1)}, u32[]{:S(2)}, u32[]{:S(2)}) %collective-permute-start.21) | collective-permute-done | bytes 262176 | tf_op jit(solution)/shard_map/ppermute | solution.py:59
  89.4 2.5 %collective-permute-done.22.r3 = bf16[256,512]{1,0:T(8,128)(2,1)S(1)} collective-permute-done((bf16[256,512]{1,0:T(8,128)(2,1)S(1)}, bf16[256,512]{1,0:T(8,128)(2,1)S(1)}, u32[]{:S(2)}, u32[]{:S(2)}) %collective-permute-start.22) | collective-permute-done | bytes 262176 | tf_op jit(solution)/shard_map/ppermute | solution.py:55
  91.8 1.5 %shard_map.55 = bf16[512,512]{1,0:T(8,128)(2,1)} custom-call(s32[512,128]{1,0:T(8,128)S(1)} %get-tuple-element.40.slot_ref, bf16[256,512]{1,0:T(8,128)(2,1)S(1)} %get-tuple-element.69.r0, bf16[256,512]{1,0:T(8,128)(2,1)S(1)} %collective-permute-done.20.r1, bf16[256,512]{1,0:T(8,128)(2,1)S(1)} %collective-permute-done.21.r2, ...), custom_call_target="tpu_custom_call" | custom-call | tf_op jit(solution)/shard_map/pallas_call | solution.py:295
  (45 shorter events, 15.8 us)
Async XLA Ops:
  0.0 3.4 %collective-permute-start.1 = (bf16[512,512]{1,0:T(8,128)(2,1)}, bf16[512,512]{1,0:T(8,128)(2,1)S(1)}, u32[]{:S(2)}, u32[]{:S(2)}) collective-permute-start(bf16[512,512]{1,0:T(8,128)(2,1)} %q_ref.1), channel_id=1, source_target_pairs={{0,1},{1,0},{2,3},{3,2},{4,5},{5,4},{6,7},{7,6},{8,9},{9,8},{10,11... | collective-permute-start | bytes 1572872 | tf_op jit(solution)/shard_map/ppermute | solution.py:46
  1.4 2.0 %collective-permute-start = (s32[1,512]{1,0:T(1,128)}, s32[1,512]{1,0:T(1,128)S(1)}, u32[]{:S(2)}, u32[]{:S(2)}) collective-permute-start(s32[1,512]{1,0:T(1,128)} %bitcast.1), channel_id=1, source_target_pairs={{0,1},{1,0},{2,3},{3,2},{4,5},{5,4},{6,7},{7,6},{8,9},{9,8},{10,11... | collective-permute-start | bytes 6152 | tf_op jit(solution)/shard_map/ppermute | solution.py:46
  3.4 1.0 %copy-start = (bf16[512,512]{1,0:T(8,128)(2,1)S(1)}, bf16[512,512]{1,0:T(8,128)(2,1)}, u32[]{:S(2)}) copy-start(bf16[512,512]{1,0:T(8,128)(2,1)} %q_ref.1) | copy-start | bytes 1572868
  6.2 13.5 %collective-permute-start.2 = (bf16[768,512]{1,0:T(8,128)(2,1)S(1)}, bf16[768,512]{1,0:T(8,128)(2,1)S(1)}, u32[]{:S(2)}, u32[]{:S(2)}) collective-permute-start(bf16[768,512]{1,0:T(8,128)(2,1)S(1)} %get-tuple-element.42), channel_id=1, source_target_pairs={{0,32},{1,97},{2,34},{3,99},{4,36},{5,101},{6,38},{7,103},{8,40},{... | collective-permute-start | bytes 2359304 | tf_op jit(solution)/shard_map/ppermute | solution.py:55
  10.1 9.6 %collective-permute-start.3 = (bf16[512,512]{1,0:T(8,128)(2,1)S(1)}, bf16[512,512]{1,0:T(8,128)(2,1)S(1)}, u32[]{:S(2)}, u32[]{:S(2)}) collective-permute-start(bf16[512,512]{1,0:T(8,128)(2,1)S(1)} %get-tuple-element.74.refs_0_), channel_id=1, source_target_pairs={{0,8},{1,3},{2,10},{3,5},{4,12},{5,7},{6,14},{7,1},{8,16},{9,11},{... | collective-permute-start | bytes 1572872 | tf_op jit(solution)/shard_map/ppermute | solution.py:38
  11.4 8.3 %collective-permute-start.4 = (bf16[512,512]{1,0:T(8,128)(2,1)S(1)}, bf16[512,512]{1,0:T(8,128)(2,1)S(1)}, u32[]{:S(2)}, u32[]{:S(2)}) collective-permute-start(bf16[512,512]{1,0:T(8,128)(2,1)S(1)} %get-tuple-element.74.refs_0_), channel_id=1, source_target_pairs={{0,24},{1,7},{2,26},{3,1},{4,28},{5,3},{6,30},{7,5},{8,0},{9,15},{... | collective-permute-start | bytes 1572872 | tf_op jit(solution)/shard_map/ppermute | solution.py:38
  19.8 6.9 %collective-permute-start.5 = (bf16[768,512]{1,0:T(8,128)(2,1)S(1)}, bf16[768,512]{1,0:T(8,128)(2,1)S(1)}, u32[]{:S(2)}, u32[]{:S(2)}) collective-permute-start(bf16[768,512]{1,0:T(8,128)(2,1)S(1)} %collective-permute-done.2.refs_4_.refs_5_.refs_3_.refs_1_), channel_id=1, source_target_pairs={{0,1},{1,0},{2,3},{3,2},{4,5},{5,4},{6,7},{7,6},{8,9},{9,8},{10,11... | collective-permute-start | bytes 2359304 | tf_op jit(solution)/shard_map/ppermute | solution.py:46
  20.9 10.1 %collective-permute-start.7 = (bf16[512,512]{1,0:T(8,128)(2,1)S(1)}, bf16[512,512]{1,0:T(8,128)(2,1)S(1)}, u32[]{:S(2)}, u32[]{:S(2)}) collective-permute-start(bf16[512,512]{1,0:T(8,128)(2,1)S(1)} %collective-permute-done.3.refs_1_), channel_id=1, source_target_pairs={{0,8},{1,3},{2,10},{3,5},{4,12},{5,7},{6,14},{7,1},{8,16},{9,11},{... | collective-permute-start | bytes 1572872 | tf_op jit(solution)/shard_map/ppermute | solution.py:38
  22.3 21.0 %collective-permute-start.17 = (bf16[1024,512]{1,0:T(8,128)(2,1)S(1)}, bf16[1024,512]{1,0:T(8,128)(2,1)S(1)}, u32[]{:S(2)}, u32[]{:S(2)}) collective-permute-start(bf16[1024,512]{1,0:T(8,128)(2,1)S(1)} %pad_maximum_fusion), channel_id=1, source_target_pairs={{0,6},{1,25},{2,0},{3,27},{4,2},{5,29},{6,4},{7,31},{8,14},{9,1},{... | collective-permute-start | bytes 3145736 | tf_op jit(solution)/shard_map/ppermute | solution.py:42
  24.8 18.5 %collective-permute-start.14 = (bf16[1024,512]{1,0:T(8,128)(2,1)S(1)}, bf16[1024,512]{1,0:T(8,128)(2,1)S(1)}, u32[]{:S(2)}, u32[]{:S(2)}) collective-permute-start(bf16[1024,512]{1,0:T(8,128)(2,1)S(1)} %pad_maximum_fusion), channel_id=1, source_target_pairs={{0,2},{1,9},{2,4},{3,11},{4,6},{5,13},{6,0},{7,15},{8,10},{9,17},{... | collective-permute-start | bytes 3145736 | tf_op jit(solution)/shard_map/ppermute | solution.py:42
  24.8 9.8 %collective-permute-start.6 = (bf16[256,512]{1,0:T(8,128)(2,1)S(1)}, bf16[256,512]{1,0:T(8,128)(2,1)S(1)}, u32[]{:S(2)}, u32[]{:S(2)}) collective-permute-start(bf16[256,512]{1,0:T(8,128)(2,1)S(1)} %slice.15), channel_id=1, source_target_pairs={{0,32},{1,97},{2,34},{3,99},{4,36},{5,101},{6,38},{7,103},{8,40},{... | collective-permute-start | bytes 786440 | tf_op jit(solution)/shard_map/ppermute | solution.py:55
  31.0 21.8 %collective-permute-start.10 = (bf16[1024,512]{1,0:T(8,128)(2,1)S(1)}, bf16[1024,512]{1,0:T(8,128)(2,1)S(1)}, u32[]{:S(2)}, u32[]{:S(2)}) collective-permute-start(bf16[1024,512]{1,0:T(8,128)(2,1)S(1)} %constant_dynamic-update-slice_fusion.2), channel_id=1, source_target_pairs={{0,6},{1,25},{2,0},{3,27},{4,2},{5,29},{6,4},{7,31},{8,14},{9,1},{... | collective-permute-start | bytes 3145736 | tf_op jit(solution)/shard_map/ppermute | solution.py:42
  34.6 21.0 %collective-permute-start.8 = (bf16[1024,512]{1,0:T(8,128)(2,1)S(1)}, bf16[1024,512]{1,0:T(8,128)(2,1)S(1)}, u32[]{:S(2)}, u32[]{:S(2)}) collective-permute-start(bf16[1024,512]{1,0:T(8,128)(2,1)S(1)} %constant_dynamic-update-slice_fusion.2), channel_id=1, source_target_pairs={{0,2},{1,9},{2,4},{3,11},{4,6},{5,13},{6,0},{7,15},{8,10},{9,17},{... | collective-permute-start | bytes 3145736 | tf_op jit(solution)/shard_map/ppermute | solution.py:42
  34.6 4.4 %collective-permute-start.15 = (bf16[256,512]{1,0:T(8,128)(2,1)S(1)}, bf16[256,512]{1,0:T(8,128)(2,1)S(1)}, u32[]{:S(2)}, u32[]{:S(2)}) collective-permute-start(bf16[256,512]{1,0:T(8,128)(2,1)S(1)} %collective-permute-done.6.refs_8_.refs_6_.refs_3_), channel_id=1, source_target_pairs={{0,1},{1,0},{2,3},{3,2},{4,5},{5,4},{6,7},{7,6},{8,9},{9,8},{10,11... | collective-permute-start | bytes 786440 | tf_op jit(solution)/shard_map/ppermute | solution.py:46
  43.3 12.6 %collective-permute-start.18 = (bf16[512,512]{1,0:T(8,128)(2,1)S(1)}, bf16[512,512]{1,0:T(8,128)(2,1)S(1)}, u32[]{:S(2)}, u32[]{:S(2)}) collective-permute-start(bf16[512,512]{1,0:T(8,128)(2,1)S(1)} %slice.19), channel_id=1, source_target_pairs={{0,6},{1,25},{2,0},{3,27},{4,2},{5,29},{6,4},{7,31},{8,14},{9,1},{... | collective-permute-start | bytes 1572872 | tf_op jit(solution)/shard_map/ppermute | solution.py:42
  46.7 12.3 %collective-permute-start.16 = (bf16[512,512]{1,0:T(8,128)(2,1)S(1)}, bf16[512,512]{1,0:T(8,128)(2,1)S(1)}, u32[]{:S(2)}, u32[]{:S(2)}) collective-permute-start(bf16[512,512]{1,0:T(8,128)(2,1)S(1)} %slice.18), channel_id=1, source_target_pairs={{0,2},{1,9},{2,4},{3,11},{4,6},{5,13},{6,0},{7,15},{8,10},{9,17},{... | collective-permute-start | bytes 1572872 | tf_op jit(solution)/shard_map/ppermute | solution.py:42
  52.8 14.4 %collective-permute-start.11 = (bf16[512,512]{1,0:T(8,128)(2,1)S(1)}, bf16[512,512]{1,0:T(8,128)(2,1)S(1)}, u32[]{:S(2)}, u32[]{:S(2)}) collective-permute-start(bf16[512,512]{1,0:T(8,128)(2,1)S(1)} %slice.21), channel_id=1, source_target_pairs={{0,6},{1,25},{2,0},{3,27},{4,2},{5,29},{6,4},{7,31},{8,14},{9,1},{... | collective-permute-start | bytes 1572872 | tf_op jit(solution)/shard_map/ppermute | solution.py:42
  55.6 9.8 %collective-permute-start.9 = (bf16[512,512]{1,0:T(8,128)(2,1)S(1)}, bf16[512,512]{1,0:T(8,128)(2,1)S(1)}, u32[]{:S(2)}, u32[]{:S(2)}) collective-permute-start(bf16[512,512]{1,0:T(8,128)(2,1)S(1)} %slice.20), channel_id=1, source_target_pairs={{0,2},{1,9},{2,4},{3,11},{4,6},{5,13},{6,0},{7,15},{8,10},{9,17},{... | collective-permute-start | bytes 1572872 | tf_op jit(solution)/shard_map/ppermute | solution.py:42
  63.2 9.0 %collective-permute-start.19 = (bf16[1024,640]{1,0:T(8,128)(2,1)S(1)}, bf16[1024,640]{1,0:T(8,128)(2,1)S(1)}, u32[]{:S(2)}, u32[]{:S(2)}) collective-permute-start(bf16[1024,640]{1,0:T(8,128)(2,1)S(1)} %shard_map.52), channel_id=1, source_target_pairs={{0,1},{1,0},{2,3},{3,2},{4,5},{5,4},{6,7},{7,6},{8,9},{9,8},{10,11... | collective-permute-start | bytes 3932168 | tf_op jit(solution)/shard_map/ppermute | solution.py:46
  65.4 8.4 %collective-permute-start.12 = (bf16[512,512]{1,0:T(8,128)(2,1)S(1)}, bf16[512,512]{1,0:T(8,128)(2,1)S(1)}, u32[]{:S(2)}, u32[]{:S(2)}) collective-permute-start(bf16[512,512]{1,0:T(8,128)(2,1)S(1)} %collective-permute-done.9.refs_4_), channel_id=1, source_target_pairs={{0,1},{1,0},{2,3},{3,2},{4,5},{5,4},{6,7},{7,6},{8,9},{9,8},{10,11... | collective-permute-start | bytes 1572872 | tf_op jit(solution)/shard_map/ppermute | solution.py:46
  67.2 6.7 %collective-permute-start.13 = (bf16[512,512]{1,0:T(8,128)(2,1)S(1)}, bf16[512,512]{1,0:T(8,128)(2,1)S(1)}, u32[]{:S(2)}, u32[]{:S(2)}) collective-permute-start(bf16[512,512]{1,0:T(8,128)(2,1)S(1)} %collective-permute-done.11.refs_5_), channel_id=1, source_target_pairs={{0,1},{1,0},{2,3},{3,2},{4,5},{5,4},{6,7},{7,6},{8,9},{9,8},{10,11... | collective-permute-start | bytes 1572872 | tf_op jit(solution)/shard_map/ppermute | solution.py:46
  76.9 6.5 %collective-permute-start.20 = (bf16[256,512]{1,0:T(8,128)(2,1)S(1)}, bf16[256,512]{1,0:T(8,128)(2,1)S(1)}, u32[]{:S(2)}, u32[]{:S(2)}) collective-permute-start(bf16[256,512]{1,0:T(8,128)(2,1)S(1)} %get-tuple-element.70), channel_id=1, source_target_pairs={{0,96},{1,33},{2,98},{3,35},{4,100},{5,37},{6,102},{7,39},{8,104},... | collective-permute-start | bytes 786440 | tf_op jit(solution)/shard_map/ppermute | solution.py:55
  77.0 12.4 %collective-permute-start.21 = (bf16[256,512]{1,0:T(8,128)(2,1)S(1)}, bf16[256,512]{1,0:T(8,128)(2,1)S(1)}, u32[]{:S(2)}, u32[]{:S(2)}) collective-permute-start(bf16[256,512]{1,0:T(8,128)(2,1)S(1)} %get-tuple-element.71), channel_id=1, source_target_pairs={{0,64},{32,96},{64,0},{96,32},{1,65},{33,97},{65,1},{97,33},{2,66}... | collective-permute-start | bytes 786440 | tf_op jit(solution)/shard_map/ppermute | solution.py:59
  80.0 11.9 %collective-permute-start.22 = (bf16[256,512]{1,0:T(8,128)(2,1)S(1)}, bf16[256,512]{1,0:T(8,128)(2,1)S(1)}, u32[]{:S(2)}, u32[]{:S(2)}) collective-permute-start(bf16[256,512]{1,0:T(8,128)(2,1)S(1)} %get-tuple-element.72), channel_id=1, source_target_pairs={{0,32},{1,97},{2,34},{3,99},{4,36},{5,101},{6,38},{7,103},{8,40},{... | collective-permute-start | bytes 786440 | tf_op jit(solution)/shard_map/ppermute | solution.py:55
  (1 other events, 0.7 us)

commit v3 on v2

--- a/solution.py
+++ b/solution.py
@@ -88,7 +88,7 @@
     return rel * CAP + rank.astype(jnp.int32)
 
 
-def dispatch_kernel(cat_ref, far_cat_ref, q_ref, far_q_ref, out0, sent, far0, slot_ref):
+def dispatch_kernel(cat_ref, far_cat_ref, q_ref, far_q_ref, out0, out1, far1, out2, far0, slot_ref):
     rows = cat_ref.shape[1]
     slot, far_slot = classes(cat_ref[...]), classes(far_cat_ref[...])
     iota = lax.broadcasted_iota(jnp.int32, (CAP, rows), 0)
@@ -96,9 +96,9 @@
     def pick(r, slots, ref):
         return nn((iota + r * CAP == slots).astype(BF), ref[...]).astype(BF)
 
-    sent[0:CAP, :] = pick(1, slot, q_ref)
-    sent[CAP : 2 * CAP, :] = pick(1, far_slot, far_q_ref)
-    sent[2 * CAP : 3 * CAP, :] = pick(2, slot, q_ref)
+    out1[...] = pick(1, slot, q_ref)
+    far1[...] = pick(1, far_slot, far_q_ref)
+    out2[...] = pick(2, slot, q_ref)
     out0[...] = pick(0, slot, q_ref)
     far0[...] = pick(0, far_slot, far_q_ref)
     column = jnp.transpose(jnp.broadcast_to(slot.astype(F32), (128, rows)))
@@ -110,10 +110,10 @@
     out = lambda n: jax.ShapeDtypeStruct((n, D), BF)
     return pl.pallas_call(
         dispatch_kernel,
-        out_shape=[out(CAP), out(3 * CAP), out(CAP)]
+        out_shape=[out(CAP)] * 5
         + [jax.ShapeDtypeStruct((rows, 128), jnp.int32)],
         in_specs=[VMEM] * 4,
-        out_specs=[VMEM] * 4,
+        out_specs=[VMEM] * 6,
         compiler_params=params(16),
     )(cats, far_cats, queries, far_queries)
 
@@ -306,16 +306,16 @@
     cats = categories.reshape(1, rows)
     here = jnp.concatenate([item_keys, item_values], axis=0)
     far_cats = after(swap_cores(cats), here)
-    q0, sent, far_q0, slots = dispatch(cats, far_cats, queries, swap_cores(queries))
+    q0, sent1, sent_far, sent2, far_q0, slots = dispatch(cats, far_cats, queries, swap_cores(queries))
     left, right = first_hop(here, 1), first_hop(here, -1)
-    q12 = after(plane_hop(sent, 1), left, right)
-    q2 = plane_hop(q12[2 * CAP :], 1)
-    far_q12 = swap_cores(q12)
-    far_q2 = swap_cores(after(q2, far_q12))
-    early = [q0, q12, far_q0, far_q12]
+    q2 = plane_hop(plane_hop(sent2, 1), 1)
+    q1, q3 = plane_hop(sent1, 1), plane_hop(sent_far, 1)
+    far_q1, far_q3 = swap_cores(q1), swap_cores(q3)
+    far_q2 = swap_cores(after(q2, far_q1, far_q3))
+    early = [q0, q1, q3, far_q0, far_q1, far_q3]
     qs = early + [q2, far_q2]
-    own = ((0, 0), (1, 0), (3, CAP), (4, 0))
-    theirs = ((2, 0), (3, 0), (1, CAP), (5, 0))
+    own = ((0, 0), (1, 0), (5, 0), (6, 0))
+    theirs = ((3, 0), (4, 0), (2, 0), (7, 0))
     tiles = own + theirs
 
     pair = after(jnp.concatenate([left, right], axis=0), slots)
@@ -333,12 +333,13 @@
     rest = jnp.concatenate([here, after(far, state[0][1])], axis=0)
     up_rest, down_rest = second_hop(rest, 1), second_hop(rest, -1)
     own_far = whole(3)
-    plan = ((((own_far,), False),) * 3 + ((first + (own_far,), True),)) * 2
-    state = fold(qs, tiles, [here, left, right, far], plan, state, weight=1)
+    plan = (((), False),) * 3 + ((first + (own_far,), True),)
+    state = fold(qs, tiles, [here, left, right, far], plan * 2, state, weight=1)
     up_pair, down_pair = after(up_pair, state[0][1]), after(down_pair, state[0][1])
     up_left, down_right = second_hop(up_pair[:two], 1), second_hop(down_pair[two:], -1)
-    both = same([whole(i, j) for i in range(2) for j in (0, two)])
-    state = fold(qs, tiles, [up_pair, down_pair], both, state, weight=1)
+    pair_blocks = tuple(whole(i, j) for i in range(2) for j in (0, two))
+    plan = ((pair_blocks + (whole(2),), False),) * 3 + ((pair_blocks, False),)
+    state = fold(qs, tiles, [up_pair, down_pair, far], plan * 2, state, weight=1)
     up_here = second_hop(up_rest[:two], 1)
     down_far = second_hop(down_rest[two:], -1)
     mine, others = state
@@ -352,8 +353,8 @@
     merged = merge(mine, other)
     last = [up_here, down_far]
     last += [swap_cores(a) for a in last]
-    mine_q = ((0, 0), (1, 0), (2, CAP), (3, 0))
-    done = finish([q0, q12, far_q12, q2], mine_q, last, merged)
+    mine_q = ((0, 0), (1, 0), (2, 0), (3, 0))
+    done = finish([q0, q1, far_q3, q2], mine_q, last, merged)
     back2 = opposite_plane(done[3])
     ahead, behind = plane_hop(done[1], -1), plane_hop(done[2], 1)
     return collect(slots, (done[0], ahead, back2, behind))

time: 94 us -> 86.3 us (0.918)
  starting transfers between devices: 34.2 us -> 31.2 us
  waiting for transfers between devices: 25.3 us -> 22.8 us
  Pallas kernels: 29.8 us -> 28 us
    ppermute x4 -> x6, waiting for transfers between devices: 5.13 us -> 14.5 us  [plane_hop(): return lax.ppermute(a, ('cat',) + PLANE, pairs)]
    ppermute x3, waiting for transfers between devices: 8.17 us -> 0.01 us  [first_hop(): return lax.ppermute(a, PLANE, hops(True, step))]
    ppermute x1, waiting for transfers between devices: 6.02 us -> 0.01 us  [opposite_plane(): return lax.ppermute(a, 'cat', [(i, (i + 2) % CATS) for i in range(CATS)])]
    ppermute x8, starting transfers between devices: 12.5 us -> 9.79 us  [second_hop(): return lax.ppermute(a, PLANE, hops(False, step))]
    pallas_call x6, Pallas kernels: 22.6 us -> 20.8 us  [fold(): pl.pallas_call(kernel, out_shape=out_shape, in_specs=[VMEM] * len(args),...]
    ppermute x8, waiting for transfers between devices: 4.77 us -> 6.04 us  [second_hop(): return lax.ppermute(a, PLANE, hops(False, step))]
    ppermute x7 -> x8, waiting for transfers between devices: 1.18 us -> 2.21 us  [swap_cores(): return lax.ppermute(a, PLANE, [(i, i ^ 1) for i in range(32)])]
    ppermute x4 -> x6, starting transfers between devices: 6.51 us -> 6.6 us  [plane_hop(): return lax.ppermute(a, ('cat',) + PLANE, pairs)]
  transfers between devices with their start and end apart: 23 -> 26, of which waited for: 8 -> 10; matrix products, arithmetic and copies ran while one was open for 2% -> 3% of each run, Pallas kernels for 26% -> 27%
where the time goes in v3:
time: 86.3 us; the launch traced here: 86.1 us
  starting transfers between devices  31.2 us (36%)
  Pallas kernels  28 us (32%)
  waiting for transfers between devices  22.8 us (26%)
  local copies, waits for them, and re-layouts  3.87 us (4%)
    pallas_call x6, Pallas kernels, fold(): pl.pallas_call(kernel, out_shape=out_shape, in_specs=[VMEM] * len(args),...  20.8 us
    ppermute x6, waiting for transfers between devices, plane_hop(): return lax.ppermute(a, ('cat',) + PLANE, pairs)  14.5 us
    ppermute x8, starting transfers between devices, second_hop(): return lax.ppermute(a, PLANE, hops(False, step))  9.79 us
    ppermute x8, starting transfers between devices, swap_cores(): return lax.ppermute(a, PLANE, [(i, i ^ 1) for i in range(32)])  8.06 us
    ppermute x6, starting transfers between devices, plane_hop(): return lax.ppermute(a, ('cat',) + PLANE, pairs)  6.6 us
    ppermute x8, waiting for transfers between devices, second_hop(): return lax.ppermute(a, PLANE, hops(False, step))  6.04 us
    ppermute x3, starting transfers between devices, first_hop(): return lax.ppermute(a, PLANE, hops(True, step))  4.26 us
    unnamed x6, local copies, waits for them, and re-layouts  3.69 us
  transfers between devices with their start and end apart: 26, of which 10 were waited for; matrix products, arithmetic and copies ran while one was open for 3% of the time, Pallas kernels for 27%

profile of v3, /device:TPU:1, one launch (start us, length us, event | category | flops | bytes accessed | tf_op | source)
XLA Modules:
  0.0 86.1 jit_solution(1230562603218748189)
XLA Ops:
  3.4 1.4 %collective-permute-start.7 = (bf16[512,512]{1,0:T(8,128)(2,1)S(1)}, bf16[512,512]{1,0:T(8,128)(2,1)S(1)}, u32[]{:S(2)}, u32[]{:S(2)}) collective-permute-start(bf16[512,512]{1,0:T(8,128)(2,1)S(1)} %get-tuple-element.76.refs_0_), channel_id=1, source_target_pairs={{0,8},{1,3},{2,10},{3,5},{4,12},{5,7},{6,14},{7,1},{8,16},{9,11},{... | collective-permute-start | bytes 1572872 | tf_op jit(solution)/shard_map/ppermute | solution.py:38
  4.9 1.5 %collective-permute-start.9 = (bf16[512,512]{1,0:T(8,128)(2,1)S(1)}, bf16[512,512]{1,0:T(8,128)(2,1)S(1)}, u32[]{:S(2)}, u32[]{:S(2)}) collective-permute-start(bf16[512,512]{1,0:T(8,128)(2,1)S(1)} %get-tuple-element.76.refs_0_), channel_id=1, source_target_pairs={{0,24},{1,7},{2,26},{3,1},{4,28},{5,3},{6,30},{7,5},{8,0},{9,15},{... | collective-permute-start | bytes 1572872 | tf_op jit(solution)/shard_map/ppermute | solution.py:38
  10.5 3.9 %collective-permute-start.2 = (bf16[256,512]{1,0:T(8,128)(2,1)S(1)}, bf16[256,512]{1,0:T(8,128)(2,1)S(1)}, u32[]{:S(2)}, u32[]{:S(2)}) collective-permute-start(bf16[256,512]{1,0:T(8,128)(2,1)S(1)} %get-tuple-element.43), channel_id=1, source_target_pairs={{0,32},{1,97},{2,34},{3,99},{4,36},{5,101},{6,38},{7,103},{8,40},{... | collective-permute-start | bytes 786440 | tf_op jit(solution)/shard_map/ppermute | solution.py:55
  18.9 1.7 %collective-permute-done.3.refs_5_.refs_6_ = bf16[256,512]{1,0:T(8,128)(2,1)S(1)} collective-permute-done((bf16[256,512]{1,0:T(8,128)(2,1)S(1)}, bf16[256,512]{1,0:T(8,128)(2,1)S(1)}, u32[]{:S(2)}, u32[]{:S(2)}) %collective-permute-start.3) | collective-permute-done | bytes 262176 | tf_op jit(solution)/shard_map/ppermute | solution.py:55
  20.6 1.7 %collective-permute-start.10 = (bf16[256,512]{1,0:T(8,128)(2,1)S(1)}, bf16[256,512]{1,0:T(8,128)(2,1)S(1)}, u32[]{:S(2)}, u32[]{:S(2)}) collective-permute-start(bf16[256,512]{1,0:T(8,128)(2,1)S(1)} %collective-permute-done.2.refs_4_.refs_5_.refs_1_), channel_id=1, source_target_pairs={{0,1},{1,0},{2,3},{3,2},{4,5},{5,4},{6,7},{7,6},{8,9},{9,8},{10,11... | collective-permute-start | bytes 786440 | tf_op jit(solution)/shard_map/ppermute | solution.py:46
  23.4 1.7 %collective-permute-start.4 = (bf16[256,512]{1,0:T(8,128)(2,1)S(1)}, bf16[256,512]{1,0:T(8,128)(2,1)S(1)}, u32[]{:S(2)}, u32[]{:S(2)}) collective-permute-start(bf16[256,512]{1,0:T(8,128)(2,1)S(1)} %collective-permute-done.3.refs_5_.refs_6_), channel_id=1, source_target_pairs={{0,1},{1,0},{2,3},{3,2},{4,5},{5,4},{6,7},{7,6},{8,9},{9,8},{10,11... | collective-permute-start | bytes 786440 | tf_op jit(solution)/shard_map/ppermute | solution.py:46
  25.0 1.8 %collective-permute-start.6 = (bf16[256,512]{1,0:T(8,128)(2,1)S(1)}, bf16[256,512]{1,0:T(8,128)(2,1)S(1)}, u32[]{:S(2)}, u32[]{:S(2)}) collective-permute-start(bf16[256,512]{1,0:T(8,128)(2,1)S(1)} %collective-permute-done.5), channel_id=1, source_target_pairs={{0,32},{1,97},{2,34},{3,99},{4,36},{5,101},{6,38},{7,103},{8,40},{... | collective-permute-start | bytes 786440 | tf_op jit(solution)/shard_map/ppermute | solution.py:55
  26.8 3.0 %shard_map.47 = (f32[1024,512]{1,0:T(8,128)S(1)}, f32[1024,128]{1,0:T(8,128)S(1)}, f32[1024,512]{1,0:T(8,128)S(1)}, f32[1024,128]{1,0:T(8,128)S(1)}) custom-call(bf16[512,512]{1,0:T(8,128)(2,1)S(1)} %get-tuple-element.76.refs_0_, bf16[512,512]{1,0:T(8,128)(2,1)S(1)} %collective-permute-done.7.refs_1_, bf16[512,512]{1,0:T(8,128)(2,1)S(1)} %collective-permute-done.9.refs_2_, ...), custom_call_target="tpu_custom_call" | custom-call | flops 724774912 | bytes 393216 | tf_op jit(solution)/shard_map/pallas_call | solution.py:211
  31.1 1.6 %collective-permute-start.13 = (bf16[1024,512]{1,0:T(8,128)(2,1)S(1)}, bf16[1024,512]{1,0:T(8,128)(2,1)S(1)}, u32[]{:S(2)}, u32[]{:S(2)}) collective-permute-start(bf16[1024,512]{1,0:T(8,128)(2,1)S(1)} %constant_dynamic-update-slice_fusion.2), channel_id=1, source_target_pairs={{0,6},{1,25},{2,0},{3,27},{4,2},{5,29},{6,4},{7,31},{8,14},{9,1},{... | collective-permute-start | bytes 3145736 | tf_op jit(solution)/shard_map/ppermute | solution.py:42
  32.7 2.4 %collective-permute-start.18 = (bf16[256,512]{1,0:T(8,128)(2,1)S(1)}, bf16[256,512]{1,0:T(8,128)(2,1)S(1)}, u32[]{:S(2)}, u32[]{:S(2)}) collective-permute-start(bf16[256,512]{1,0:T(8,128)(2,1)S(1)} %collective-permute-done.6.refs_10_.refs_9_.refs_3_), channel_id=1, source_target_pairs={{0,1},{1,0},{2,3},{3,2},{4,5},{5,4},{6,7},{7,6},{8,9},{9,8},{10,11... | collective-permute-start | bytes 786440 | tf_op jit(solution)/shard_map/ppermute | solution.py:46
  36.2 1.8 %shard_map.48 = (f32[1024,512]{1,0:T(8,128)S(1)}, f32[1024,128]{1,0:T(8,128)S(1)}, f32[1024,512]{1,0:T(8,128)S(1)}, f32[1024,128]{1,0:T(8,128)S(1)}) custom-call(bf16[512,512]{1,0:T(8,128)(2,1)S(1)} %get-tuple-element.76.refs_0_, ...), custom_call_target="tpu_custom_call", output_to_operand_aliasing={{0}: (12, {}), {1}: (13, {}), {2}: (14, {}), {3}: (15, {})} | custom-call | flops 1073741824 | bytes 524288 | tf_op jit(solution)/shard_map/pallas_call | solution.py:211
  39.9 6.7 %shard_map.49 = (f32[1024,512]{1,0:T(8,128)S(1)}, f32[1024,128]{1,0:T(8,128)S(1)}, f32[1024,512]{1,0:T(8,128)S(1)}, f32[1024,128]{1,0:T(8,128)S(1)}) custom-call(bf16[1024,512]{1,0:T(8,128)(2,1)S(1)} %collective-permute-done.17.refs_0_, ...), custom_call_target="tpu_custom_call", output_to_operand_aliasing={{0}: (11, {}), {1}: (12, {}), {2}: (13, {}), {3}: (14, {})} | custom-call | flops 5100273664 | bytes 393216 | tf_op jit(solution)/shard_map/pallas_call | solution.py:211
  46.6 2.3 %collective-permute-done.11.refs_0_ = bf16[1024,512]{1,0:T(8,128)(2,1)S(1)} collective-permute-done((bf16[1024,512]{1,0:T(8,128)(2,1)S(1)}, bf16[1024,512]{1,0:T(8,128)(2,1)S(1)}, u32[]{:S(2)}, u32[]{:S(2)}) %collective-permute-start.11) | collective-permute-done | bytes 1048608 | tf_op jit(solution)/shard_map/ppermute | solution.py:42
  49.1 2.7 %collective-permute-start.14 = (bf16[512,512]{1,0:T(8,128)(2,1)S(1)}, bf16[512,512]{1,0:T(8,128)(2,1)S(1)}, u32[]{:S(2)}, u32[]{:S(2)}) collective-permute-start(bf16[512,512]{1,0:T(8,128)(2,1)S(1)} %slice.17), channel_id=1, source_target_pairs={{0,6},{1,25},{2,0},{3,27},{4,2},{5,29},{6,4},{7,31},{8,14},{9,1},{... | collective-permute-start | bytes 1572872 | tf_op jit(solution)/shard_map/ppermute | solution.py:42
  51.9 2.7 %collective-permute-done.19.refs_2_ = bf16[512,512]{1,0:T(8,128)(2,1)S(1)} collective-permute-done((bf16[512,512]{1,0:T(8,128)(2,1)S(1)}, bf16[512,512]{1,0:T(8,128)(2,1)S(1)}, u32[]{:S(2)}, u32[]{:S(2)}) %collective-permute-start.19) | collective-permute-done | bytes 524320 | tf_op jit(solution)/shard_map/ppermute | solution.py:42
  54.6 4.2 %shard_map.52 = bf16[1024,640]{1,0:T(8,128)(2,1)S(1)} custom-call(bf16[1024,512]{1,0:T(8,128)(2,1)S(1)} %collective-permute-done.11.refs_0_, bf16[1024,512]{1,0:T(8,128)(2,1)S(1)} %collective-permute-done.13.refs_1_, bf16[512,512]{1,0:T(8,128)(2,1)S(1)} %collective-permute-done.19.refs_2_, bf16[512,512]{1,0:T(8,128)(2,1)S(1)} %collective-permute-done.21.refs_3_, ...), custom_call_target="tpu_custom_call" | custom-call | flops 9663676416 | bytes 524288 | tf_op jit(solution)/shard_map/pallas_call | solution.py:211
  60.4 2.5 %shard_map.50 = (f32[1024,512]{1,0:T(8,128)S(1)}, f32[1024,128]{1,0:T(8,128)S(1)}) custom-call(bf16[1024,512]{1,0:T(8,128)(2,1)S(1)} %collective-permute-done.11.refs_0_, bf16[1024,512]{1,0:T(8,128)(2,1)S(1)} %collective-permute-done.13.refs_1_, ...), custom_call_target="tpu_custom_call", output_to_operand_aliasing={{0}: (12, {}), {1}: (13, {})} | custom-call | flops 4831838208 | bytes 524288 | tf_op jit(solution)/shard_map/pallas_call | solution.py:211
  62.9 2.5 %shard_map.51 = (f32[1024,512]{1,0:T(8,128)S(1)}, f32[1024,128]{1,0:T(8,128)S(1)}) custom-call(bf16[1024,512]{1,0:T(8,128)(2,1)S(1)} %collective-permute-done.11.refs_0_, bf16[1024,512]{1,0:T(8,128)(2,1)S(1)} %collective-permute-done.13.refs_1_, ...), custom_call_target="tpu_custom_call", output_to_operand_aliasing={{0}: (12, {}), {1}: (13, {})} | custom-call | flops 4831838208 | bytes 524288 | tf_op jit(solution)/shard_map/pallas_call | solution.py:211
  65.5 1.6 %shard_map.53 = (f32[1024,512]{1,0:T(8,128)S(1)}, f32[1024,128]{1,0:T(8,128)S(1)}) custom-call(f32[1024,512]{1,0:T(8,128)S(1)} %get-tuple-element.65.acc, f32[1024,128]{1,0:T(8,128)S(1)} %get-tuple-element.66.ml, bf16[1024,640]{1,0:T(8,128)(2,1)S(1)} %collective-permute-done.22.other), custom_call_target="tpu_custom_call", output_to_operand_aliasing={{0}: (0, {}), {1}: (1, {})} | custom-call | tf_op jit(solution)/shard_map/pallas_call | solution.py:240
  67.1 3.0 %shard_map.54 = (bf16[256,512]{1,0:T(8,128)(2,1)S(1)}, bf16[256,512]{1,0:T(8,128)(2,1)S(1)}, bf16[256,512]{1,0:T(8,128)(2,1)S(1)}, bf16[256,512]{1,0:T(8,128)(2,1)S(1)}) custom-call(bf16[256,512]{1,0:T(8,128)(2,1)S(1)} %get-tuple-element.42.refs_3_.refs_4_.refs_0_, bf16[256,512]{1,0:T(8,128)(2,1)S(1)} %collective-permute-done.2.refs_4_.refs_5_.refs_1_, ...), custom_call_target="tpu_custom_call" | custom-call | tf_op jit(solution)/shard_map/pallas_call | solution.py:272
  70.2 2.5 %collective-permute-start.24 = (bf16[256,512]{1,0:T(8,128)(2,1)S(1)}, bf16[256,512]{1,0:T(8,128)(2,1)S(1)}, u32[]{:S(2)}, u32[]{:S(2)}) collective-permute-start(bf16[256,512]{1,0:T(8,128)(2,1)S(1)} %get-tuple-element.73), channel_id=1, source_target_pairs={{0,64},{32,96},{64,0},{96,32},{1,65},{33,97},{65,1},{97,33},{2,66}... | collective-permute-start | bytes 786440 | tf_op jit(solution)/shard_map/ppermute | solution.py:59
  73.3 9.4 %collective-permute-done.23.r1 = bf16[256,512]{1,0:T(8,128)(2,1)S(1)} collective-permute-done((bf16[256,512]{1,0:T(8,128)(2,1)S(1)}, bf16[256,512]{1,0:T(8,128)(2,1)S(1)}, u32[]{:S(2)}, u32[]{:S(2)}) %collective-permute-start.23) | collective-permute-done | bytes 262176 | tf_op jit(solution)/shard_map/ppermute | solution.py:55
  82.7 1.9 %collective-permute-done.25.r3 = bf16[256,512]{1,0:T(8,128)(2,1)S(1)} collective-permute-done((bf16[256,512]{1,0:T(8,128)(2,1)S(1)}, bf16[256,512]{1,0:T(8,128)(2,1)S(1)}, u32[]{:S(2)}, u32[]{:S(2)}) %collective-permute-start.25) | collective-permute-done | bytes 262176 | tf_op jit(solution)/shard_map/ppermute | solution.py:55
  84.6 1.5 %shard_map.55 = bf16[512,512]{1,0:T(8,128)(2,1)} custom-call(s32[512,128]{1,0:T(8,128)S(1)} %get-tuple-element.41.slot_ref, bf16[256,512]{1,0:T(8,128)(2,1)S(1)} %get-tuple-element.71.r0, bf16[256,512]{1,0:T(8,128)(2,1)S(1)} %collective-permute-done.23.r1, bf16[256,512]{1,0:T(8,128)(2,1)S(1)} %collective-permute-done.24.r2, ...), custom_call_target="tpu_custom_call" | custom-call | tf_op jit(solution)/shard_map/pallas_call | solution.py:295
  (50 shorter events, 19.9 us)
Async XLA Ops:
  0.0 7.7 %collective-permute-start.1 = (bf16[512,512]{1,0:T(8,128)(2,1)}, bf16[512,512]{1,0:T(8,128)(2,1)S(1)}, u32[]{:S(2)}, u32[]{:S(2)}) collective-permute-start(bf16[512,512]{1,0:T(8,128)(2,1)} %q_ref.1), channel_id=1, source_target_pairs={{0,1},{1,0},{2,3},{3,2},{4,5},{5,4},{6,7},{7,6},{8,9},{9,8},{10,11... | collective-permute-start | bytes 1572872 | tf_op jit(solution)/shard_map/ppermute | solution.py:46
  3.4 11.2 %collective-permute-start.7 = (bf16[512,512]{1,0:T(8,128)(2,1)S(1)}, bf16[512,512]{1,0:T(8,128)(2,1)S(1)}, u32[]{:S(2)}, u32[]{:S(2)}) collective-permute-start(bf16[512,512]{1,0:T(8,128)(2,1)S(1)} %get-tuple-element.76.refs_0_), channel_id=1, source_target_pairs={{0,8},{1,3},{2,10},{3,5},{4,12},{5,7},{6,14},{7,1},{8,16},{9,11},{... | collective-permute-start | bytes 1572872 | tf_op jit(solution)/shard_map/ppermute | solution.py:38
  4.9 11.1 %collective-permute-start.9 = (bf16[512,512]{1,0:T(8,128)(2,1)S(1)}, bf16[512,512]{1,0:T(8,128)(2,1)S(1)}, u32[]{:S(2)}, u32[]{:S(2)}) collective-permute-start(bf16[512,512]{1,0:T(8,128)(2,1)S(1)} %get-tuple-element.76.refs_0_), channel_id=1, source_target_pairs={{0,24},{1,7},{2,26},{3,1},{4,28},{5,3},{6,30},{7,5},{8,0},{9,15},{... | collective-permute-start | bytes 1572872 | tf_op jit(solution)/shard_map/ppermute | solution.py:38
  10.5 7.2 %collective-permute-start.2 = (bf16[256,512]{1,0:T(8,128)(2,1)S(1)}, bf16[256,512]{1,0:T(8,128)(2,1)S(1)}, u32[]{:S(2)}, u32[]{:S(2)}) collective-permute-start(bf16[256,512]{1,0:T(8,128)(2,1)S(1)} %get-tuple-element.43), channel_id=1, source_target_pairs={{0,32},{1,97},{2,34},{3,99},{4,36},{5,101},{6,38},{7,103},{8,40},{... | collective-permute-start | bytes 786440 | tf_op jit(solution)/shard_map/ppermute | solution.py:55
  14.4 6.1 %collective-permute-start.3 = (bf16[256,512]{1,0:T(8,128)(2,1)S(1)}, bf16[256,512]{1,0:T(8,128)(2,1)S(1)}, u32[]{:S(2)}, u32[]{:S(2)}) collective-permute-start(bf16[256,512]{1,0:T(8,128)(2,1)S(1)} %get-tuple-element.44), channel_id=1, source_target_pairs={{0,32},{1,97},{2,34},{3,99},{4,36},{5,101},{6,38},{7,103},{8,40},{... | collective-permute-start | bytes 786440 | tf_op jit(solution)/shard_map/ppermute | solution.py:55
  14.6 8.8 %collective-permute-start.5 = (bf16[256,512]{1,0:T(8,128)(2,1)S(1)}, bf16[256,512]{1,0:T(8,128)(2,1)S(1)}, u32[]{:S(2)}, u32[]{:S(2)}) collective-permute-start(bf16[256,512]{1,0:T(8,128)(2,1)S(1)} %get-tuple-element.45), channel_id=1, source_target_pairs={{0,32},{1,97},{2,34},{3,99},{4,36},{5,101},{6,38},{7,103},{8,40},{... | collective-permute-start | bytes 786440 | tf_op jit(solution)/shard_map/ppermute | solution.py:55
  14.7 15.2 %collective-permute-start.8 = (bf16[512,512]{1,0:T(8,128)(2,1)S(1)}, bf16[512,512]{1,0:T(8,128)(2,1)S(1)}, u32[]{:S(2)}, u32[]{:S(2)}) collective-permute-start(bf16[512,512]{1,0:T(8,128)(2,1)S(1)} %collective-permute-done.7.refs_1_), channel_id=1, source_target_pairs={{0,8},{1,3},{2,10},{3,5},{4,12},{5,7},{6,14},{7,1},{8,16},{9,11},{... | collective-permute-start | bytes 1572872 | tf_op jit(solution)/shard_map/ppermute | solution.py:38
  16.0 22.0 %collective-permute-start.20 = (bf16[1024,512]{1,0:T(8,128)(2,1)S(1)}, bf16[1024,512]{1,0:T(8,128)(2,1)S(1)}, u32[]{:S(2)}, u32[]{:S(2)}) collective-permute-start(bf16[1024,512]{1,0:T(8,128)(2,1)S(1)} %pad_maximum_fusion), channel_id=1, source_target_pairs={{0,6},{1,25},{2,0},{3,27},{4,2},{5,29},{6,4},{7,31},{8,14},{9,1},{... | collective-permute-start | bytes 3145736 | tf_op jit(solution)/shard_map/ppermute | solution.py:42
  17.8 20.3 %collective-permute-start.17 = (bf16[1024,512]{1,0:T(8,128)(2,1)S(1)}, bf16[1024,512]{1,0:T(8,128)(2,1)S(1)}, u32[]{:S(2)}, u32[]{:S(2)}) collective-permute-start(bf16[1024,512]{1,0:T(8,128)(2,1)S(1)} %pad_maximum_fusion), channel_id=1, source_target_pairs={{0,2},{1,9},{2,4},{3,11},{4,6},{5,13},{6,0},{7,15},{8,10},{9,17},{... | collective-permute-start | bytes 3145736 | tf_op jit(solution)/shard_map/ppermute | solution.py:42
  20.6 4.5 %collective-permute-start.10 = (bf16[256,512]{1,0:T(8,128)(2,1)S(1)}, bf16[256,512]{1,0:T(8,128)(2,1)S(1)}, u32[]{:S(2)}, u32[]{:S(2)}) collective-permute-start(bf16[256,512]{1,0:T(8,128)(2,1)S(1)} %collective-permute-done.2.refs_4_.refs_5_.refs_1_), channel_id=1, source_target_pairs={{0,1},{1,0},{2,3},{3,2},{4,5},{5,4},{6,7},{7,6},{8,9},{9,8},{10,11... | collective-permute-start | bytes 786440 | tf_op jit(solution)/shard_map/ppermute | solution.py:46
  25.0 7.6 %collective-permute-start.6 = (bf16[256,512]{1,0:T(8,128)(2,1)S(1)}, bf16[256,512]{1,0:T(8,128)(2,1)S(1)}, u32[]{:S(2)}, u32[]{:S(2)}) collective-permute-start(bf16[256,512]{1,0:T(8,128)(2,1)S(1)} %collective-permute-done.5), channel_id=1, source_target_pairs={{0,32},{1,97},{2,34},{3,99},{4,36},{5,101},{6,38},{7,103},{8,40},{... | collective-permute-start | bytes 786440 | tf_op jit(solution)/shard_map/ppermute | solution.py:55
  29.9 19.0 %collective-permute-start.11 = (bf16[1024,512]{1,0:T(8,128)(2,1)S(1)}, bf16[1024,512]{1,0:T(8,128)(2,1)S(1)}, u32[]{:S(2)}, u32[]{:S(2)}) collective-permute-start(bf16[1024,512]{1,0:T(8,128)(2,1)S(1)} %constant_dynamic-update-slice_fusion.2), channel_id=1, source_target_pairs={{0,2},{1,9},{2,4},{3,11},{4,6},{5,13},{6,0},{7,15},{8,10},{9,17},{... | collective-permute-start | bytes 3145736 | tf_op jit(solution)/shard_map/ppermute | solution.py:42
  31.1 18.0 %collective-permute-start.13 = (bf16[1024,512]{1,0:T(8,128)(2,1)S(1)}, bf16[1024,512]{1,0:T(8,128)(2,1)S(1)}, u32[]{:S(2)}, u32[]{:S(2)}) collective-permute-start(bf16[1024,512]{1,0:T(8,128)(2,1)S(1)} %constant_dynamic-update-slice_fusion.2), channel_id=1, source_target_pairs={{0,6},{1,25},{2,0},{3,27},{4,2},{5,29},{6,4},{7,31},{8,14},{9,1},{... | collective-permute-start | bytes 3145736 | tf_op jit(solution)/shard_map/ppermute | solution.py:42
  32.7 3.6 %collective-permute-start.18 = (bf16[256,512]{1,0:T(8,128)(2,1)S(1)}, bf16[256,512]{1,0:T(8,128)(2,1)S(1)}, u32[]{:S(2)}, u32[]{:S(2)}) collective-permute-start(bf16[256,512]{1,0:T(8,128)(2,1)S(1)} %collective-permute-done.6.refs_10_.refs_9_.refs_3_), channel_id=1, source_target_pairs={{0,1},{1,0},{2,3},{3,2},{4,5},{5,4},{6,7},{7,6},{8,9},{9,8},{10,11... | collective-permute-start | bytes 786440 | tf_op jit(solution)/shard_map/ppermute | solution.py:46
  38.1 13.8 %collective-permute-start.21 = (bf16[512,512]{1,0:T(8,128)(2,1)S(1)}, bf16[512,512]{1,0:T(8,128)(2,1)S(1)}, u32[]{:S(2)}, u32[]{:S(2)}) collective-permute-start(bf16[512,512]{1,0:T(8,128)(2,1)S(1)} %slice.15), channel_id=1, source_target_pairs={{0,6},{1,25},{2,0},{3,27},{4,2},{5,29},{6,4},{7,31},{8,14},{9,1},{... | collective-permute-start | bytes 1572872 | tf_op jit(solution)/shard_map/ppermute | solution.py:42
  39.0 15.6 %collective-permute-start.19 = (bf16[512,512]{1,0:T(8,128)(2,1)S(1)}, bf16[512,512]{1,0:T(8,128)(2,1)S(1)}, u32[]{:S(2)}, u32[]{:S(2)}) collective-permute-start(bf16[512,512]{1,0:T(8,128)(2,1)S(1)} %slice.14), channel_id=1, source_target_pairs={{0,2},{1,9},{2,4},{3,11},{4,6},{5,13},{6,0},{7,15},{8,10},{9,17},{... | collective-permute-start | bytes 1572872 | tf_op jit(solution)/shard_map/ppermute | solution.py:42
  49.0 10.9 %collective-permute-start.12 = (bf16[512,512]{1,0:T(8,128)(2,1)S(1)}, bf16[512,512]{1,0:T(8,128)(2,1)S(1)}, u32[]{:S(2)}, u32[]{:S(2)}) collective-permute-start(bf16[512,512]{1,0:T(8,128)(2,1)S(1)} %slice.16), channel_id=1, source_target_pairs={{0,2},{1,9},{2,4},{3,11},{4,6},{5,13},{6,0},{7,15},{8,10},{9,17},{... | collective-permute-start | bytes 1572872 | tf_op jit(solution)/shard_map/ppermute | solution.py:42
  49.1 10.8 %collective-permute-start.14 = (bf16[512,512]{1,0:T(8,128)(2,1)S(1)}, bf16[512,512]{1,0:T(8,128)(2,1)S(1)}, u32[]{:S(2)}, u32[]{:S(2)}) collective-permute-start(bf16[512,512]{1,0:T(8,128)(2,1)S(1)} %slice.17), channel_id=1, source_target_pairs={{0,6},{1,25},{2,0},{3,27},{4,2},{5,29},{6,4},{7,31},{8,14},{9,1},{... | collective-permute-start | bytes 1572872 | tf_op jit(solution)/shard_map/ppermute | solution.py:42
  58.8 6.6 %collective-permute-start.22 = (bf16[1024,640]{1,0:T(8,128)(2,1)S(1)}, bf16[1024,640]{1,0:T(8,128)(2,1)S(1)}, u32[]{:S(2)}, u32[]{:S(2)}) collective-permute-start(bf16[1024,640]{1,0:T(8,128)(2,1)S(1)} %shard_map.52), channel_id=1, source_target_pairs={{0,1},{1,0},{2,3},{3,2},{4,5},{5,4},{6,7},{7,6},{8,9},{9,8},{10,11... | collective-permute-start | bytes 3932168 | tf_op jit(solution)/shard_map/ppermute | solution.py:46
  59.9 7.2 %collective-permute-start.15 = (bf16[512,512]{1,0:T(8,128)(2,1)S(1)}, bf16[512,512]{1,0:T(8,128)(2,1)S(1)}, u32[]{:S(2)}, u32[]{:S(2)}) collective-permute-start(bf16[512,512]{1,0:T(8,128)(2,1)S(1)} %collective-permute-done.12.refs_4_), channel_id=1, source_target_pairs={{0,1},{1,0},{2,3},{3,2},{4,5},{5,4},{6,7},{7,6},{8,9},{9,8},{10,11... | collective-permute-start | bytes 1572872 | tf_op jit(solution)/shard_map/ppermute | solution.py:46
  59.9 7.2 %collective-permute-start.16 = (bf16[512,512]{1,0:T(8,128)(2,1)S(1)}, bf16[512,512]{1,0:T(8,128)(2,1)S(1)}, u32[]{:S(2)}, u32[]{:S(2)}) collective-permute-start(bf16[512,512]{1,0:T(8,128)(2,1)S(1)} %collective-permute-done.14.refs_5_), channel_id=1, source_target_pairs={{0,1},{1,0},{2,3},{3,2},{4,5},{5,4},{6,7},{7,6},{8,9},{9,8},{10,11... | collective-permute-start | bytes 1572872 | tf_op jit(solution)/shard_map/ppermute | solution.py:46
  70.1 12.6 %collective-permute-start.23 = (bf16[256,512]{1,0:T(8,128)(2,1)S(1)}, bf16[256,512]{1,0:T(8,128)(2,1)S(1)}, u32[]{:S(2)}, u32[]{:S(2)}) collective-permute-start(bf16[256,512]{1,0:T(8,128)(2,1)S(1)} %get-tuple-element.72), channel_id=1, source_target_pairs={{0,96},{1,33},{2,98},{3,35},{4,100},{5,37},{6,102},{7,39},{8,104},... | collective-permute-start | bytes 786440 | tf_op jit(solution)/shard_map/ppermute | solution.py:55
  70.2 12.5 %collective-permute-start.24 = (bf16[256,512]{1,0:T(8,128)(2,1)S(1)}, bf16[256,512]{1,0:T(8,128)(2,1)S(1)}, u32[]{:S(2)}, u32[]{:S(2)}) collective-permute-start(bf16[256,512]{1,0:T(8,128)(2,1)S(1)} %get-tuple-element.73), channel_id=1, source_target_pairs={{0,64},{32,96},{64,0},{96,32},{1,65},{33,97},{65,1},{97,33},{2,66}... | collective-permute-start | bytes 786440 | tf_op jit(solution)/shard_map/ppermute | solution.py:59
  72.7 11.9 %collective-permute-start.25 = (bf16[256,512]{1,0:T(8,128)(2,1)S(1)}, bf16[256,512]{1,0:T(8,128)(2,1)S(1)}, u32[]{:S(2)}, u32[]{:S(2)}) collective-permute-start(bf16[256,512]{1,0:T(8,128)(2,1)S(1)} %get-tuple-element.74), channel_id=1, source_target_pairs={{0,32},{1,97},{2,34},{3,99},{4,36},{5,101},{6,38},{7,103},{8,40},{... | collective-permute-start | bytes 786440 | tf_op jit(solution)/shard_map/ppermute | solution.py:55
  (4 other events, 6.5 us)

commit v4 on v3

--- a/solution.py
+++ b/solution.py
@@ -304,8 +304,8 @@
 def shards(queries, categories, item_keys, item_values):
     rows = queries.shape[0]
     cats = categories.reshape(1, rows)
-    here = jnp.concatenate([item_keys, item_values], axis=0)
-    far_cats = after(swap_cores(cats), here)
+    far_cats = swap_cores(cats)
+    here = after(jnp.concatenate([item_keys, item_values], axis=0), far_cats)
     q0, sent1, sent_far, sent2, far_q0, slots = dispatch(cats, far_cats, queries, swap_cores(queries))
     left, right = first_hop(here, 1), first_hop(here, -1)
     q2 = plane_hop(plane_hop(sent2, 1), 1)

time: 86.3 us -> 84.9 us (0.984)
  waiting for transfers between devices: 22.8 us -> 19.5 us
  starting transfers between devices: 31.2 us -> 33.9 us
  local copies, waits for them, and re-layouts: 3.87 us -> 1.94 us
  other arithmetic: 0.07 us -> 1.13 us
    ppermute x6, waiting for transfers between devices: 14.5 us -> 5.96 us  [plane_hop(): return lax.ppermute(a, ('cat',) + PLANE, pairs)]
    ppermute x1, waiting for transfers between devices: 0.01 us -> 6.96 us  [opposite_plane(): return lax.ppermute(a, 'cat', [(i, (i + 2) % CATS) for i in range(CATS)])]
    unnamed x6 -> x5, local copies, waits for them, and re-layouts: 3.69 us -> 1.76 us
    ppermute x8, starting transfers between devices: 8.06 us -> 9.45 us  [swap_cores(): return lax.ppermute(a, PLANE, [(i, i ^ 1) for i in range(32)])]
    ppermute x3, starting transfers between devices: 4.26 us -> 2.97 us  [first_hop(): return lax.ppermute(a, PLANE, hops(True, step))]
    ppermute x8, starting transfers between devices: 9.79 us -> 11.1 us  [second_hop(): return lax.ppermute(a, PLANE, hops(False, step))]
    concatenate x0 -> x1, other arithmetic: none -> 1.06 us  [shards(): here = after(jnp.concatenate([item_keys, item_values], axis=0), far_cats)]
    ppermute x8, waiting for transfers between devices: 2.21 us -> 1.18 us  [swap_cores(): return lax.ppermute(a, PLANE, [(i, i ^ 1) for i in range(32)])]
  transfers between devices with their start and end apart: 26 -> 26, of which waited for: 10 -> 10; matrix products, arithmetic and copies ran while one was open for 3% -> 2% of each run, Pallas kernels for 27% -> 28%
where the time goes in v4:
time: 84.9 us; the launch traced here: 84.7 us
  starting transfers between devices  33.9 us (40%)
  Pallas kernels  28 us (33%)
  waiting for transfers between devices  19.5 us (23%)
  local copies, waits for them, and re-layouts  1.94 us (2%)
  other arithmetic  1.13 us (1%)
    pallas_call x6, Pallas kernels, fold(): pl.pallas_call(kernel, out_shape=out_shape, in_specs=[VMEM] * len(args),...  20.8 us
    ppermute x8, starting transfers between devices, second_hop(): return lax.ppermute(a, PLANE, hops(False, step))  11.1 us
    ppermute x8, starting transfers between devices, swap_cores(): return lax.ppermute(a, PLANE, [(i, i ^ 1) for i in range(32)])  9.45 us
    ppermute x6, starting transfers between devices, plane_hop(): return lax.ppermute(a, ('cat',) + PLANE, pairs)  7.1 us
    ppermute x1, waiting for transfers between devices, opposite_plane(): return lax.ppermute(a, 'cat', [(i, (i + 2) % CATS) for i in range(CATS)])  6.96 us
    ppermute x6, waiting for transfers between devices, plane_hop(): return lax.ppermute(a, ('cat',) + PLANE, pairs)  5.96 us
    ppermute x8, waiting for transfers between devices, second_hop(): return lax.ppermute(a, PLANE, hops(False, step))  5.4 us
    ppermute x1, starting transfers between devices, opposite_plane(): return lax.ppermute(a, 'cat', [(i, (i + 2) % CATS) for i in range(CATS)])  3.3 us
  transfers between devices with their start and end apart: 26, of which 10 were waited for; matrix products, arithmetic and copies ran while one was open for 2% of the time, Pallas kernels for 28%

profile of v4, /device:TPU:1, one launch (start us, length us, event | category | flops | bytes accessed | tf_op | source)
XLA Modules:
  0.0 84.7 jit_solution(4141653723478471721)
XLA Ops:
  4.0 1.5 %collective-permute-start.9 = (bf16[512,512]{1,0:T(8,128)(2,1)S(1)}, bf16[512,512]{1,0:T(8,128)(2,1)S(1)}, u32[]{:S(2)}, u32[]{:S(2)}) collective-permute-start(bf16[512,512]{1,0:T(8,128)(2,1)S(1)} %pad_maximum_fusion.1.refs_0_), channel_id=1, source_target_pairs={{0,24},{1,7},{2,26},{3,1},{4,28},{5,3},{6,30},{7,5},{8,0},{9,15},{... | collective-permute-start | bytes 1572872 | tf_op jit(solution)/shard_map/ppermute | solution.py:38
  8.3 3.8 %collective-permute-start.2 = (bf16[256,512]{1,0:T(8,128)(2,1)S(1)}, bf16[256,512]{1,0:T(8,128)(2,1)S(1)}, u32[]{:S(2)}, u32[]{:S(2)}) collective-permute-start(bf16[256,512]{1,0:T(8,128)(2,1)S(1)} %get-tuple-element.42), channel_id=1, source_target_pairs={{0,32},{1,97},{2,34},{3,99},{4,36},{5,101},{6,38},{7,103},{8,40},{... | collective-permute-start | bytes 786440 | tf_op jit(solution)/shard_map/ppermute | solution.py:55
  12.4 2.5 %collective-permute-start.20 = (bf16[1024,512]{1,0:T(8,128)(2,1)S(1)}, bf16[1024,512]{1,0:T(8,128)(2,1)S(1)}, u32[]{:S(2)}, u32[]{:S(2)}) collective-permute-start(bf16[1024,512]{1,0:T(8,128)(2,1)S(1)} %pad_maximum_fusion), channel_id=1, source_target_pairs={{0,6},{1,25},{2,0},{3,27},{4,2},{5,29},{6,4},{7,31},{8,14},{9,1},{... | collective-permute-start | bytes 3145736 | tf_op jit(solution)/shard_map/ppermute | solution.py:42
  16.6 1.6 %collective-permute-done.3.refs_5_.refs_6_ = bf16[256,512]{1,0:T(8,128)(2,1)S(1)} collective-permute-done((bf16[256,512]{1,0:T(8,128)(2,1)S(1)}, bf16[256,512]{1,0:T(8,128)(2,1)S(1)}, u32[]{:S(2)}, u32[]{:S(2)}) %collective-permute-start.3) | collective-permute-done | bytes 262176 | tf_op jit(solution)/shard_map/ppermute | solution.py:55
  18.2 2.2 %collective-permute-start.10 = (bf16[256,512]{1,0:T(8,128)(2,1)S(1)}, bf16[256,512]{1,0:T(8,128)(2,1)S(1)}, u32[]{:S(2)}, u32[]{:S(2)}) collective-permute-start(bf16[256,512]{1,0:T(8,128)(2,1)S(1)} %collective-permute-done.2.refs_4_.refs_5_.refs_1_), channel_id=1, source_target_pairs={{0,1},{1,0},{2,3},{3,2},{4,5},{5,4},{6,7},{7,6},{8,9},{9,8},{10,11... | collective-permute-start | bytes 786440 | tf_op jit(solution)/shard_map/ppermute | solution.py:46
  21.0 2.2 %collective-permute-start.4 = (bf16[256,512]{1,0:T(8,128)(2,1)S(1)}, bf16[256,512]{1,0:T(8,128)(2,1)S(1)}, u32[]{:S(2)}, u32[]{:S(2)}) collective-permute-start(bf16[256,512]{1,0:T(8,128)(2,1)S(1)} %collective-permute-done.3.refs_5_.refs_6_), channel_id=1, source_target_pairs={{0,1},{1,0},{2,3},{3,2},{4,5},{5,4},{6,7},{7,6},{8,9},{9,8},{10,11... | collective-permute-start | bytes 786440 | tf_op jit(solution)/shard_map/ppermute | solution.py:46
  23.3 1.8 %collective-permute-start.6 = (bf16[256,512]{1,0:T(8,128)(2,1)S(1)}, bf16[256,512]{1,0:T(8,128)(2,1)S(1)}, u32[]{:S(2)}, u32[]{:S(2)}) collective-permute-start(bf16[256,512]{1,0:T(8,128)(2,1)S(1)} %collective-permute-done.5), channel_id=1, source_target_pairs={{0,32},{1,97},{2,34},{3,99},{4,36},{5,101},{6,38},{7,103},{8,40},{... | collective-permute-start | bytes 786440 | tf_op jit(solution)/shard_map/ppermute | solution.py:55
  25.1 3.1 %shard_map.47 = (f32[1024,512]{1,0:T(8,128)S(1)}, f32[1024,128]{1,0:T(8,128)S(1)}, f32[1024,512]{1,0:T(8,128)S(1)}, f32[1024,128]{1,0:T(8,128)S(1)}) custom-call(bf16[512,512]{1,0:T(8,128)(2,1)S(1)} %pad_maximum_fusion.1.refs_0_, bf16[512,512]{1,0:T(8,128)(2,1)S(1)} %collective-permute-done.7.refs_1_, bf16[512,512]{1,0:T(8,128)(2,1)S(1)} %collective-permute-done.9.refs_2_, ...), custom_call_target="tpu_custom_call" | custom-call | flops 724774912 | bytes 393216 | tf_op jit(solution)/shard_map/pallas_call | solution.py:211
  28.6 2.3 %collective-permute-start.13 = (bf16[1024,512]{1,0:T(8,128)(2,1)S(1)}, bf16[1024,512]{1,0:T(8,128)(2,1)S(1)}, u32[]{:S(2)}, u32[]{:S(2)}) collective-permute-start(bf16[1024,512]{1,0:T(8,128)(2,1)S(1)} %constant_dynamic-update-slice_fusion), channel_id=1, source_target_pairs={{0,6},{1,25},{2,0},{3,27},{4,2},{5,29},{6,4},{7,31},{8,14},{9,1},{... | collective-permute-start | bytes 3145736 | tf_op jit(solution)/shard_map/ppermute | solution.py:42
  31.0 2.9 %collective-permute-start.18 = (bf16[256,512]{1,0:T(8,128)(2,1)S(1)}, bf16[256,512]{1,0:T(8,128)(2,1)S(1)}, u32[]{:S(2)}, u32[]{:S(2)}) collective-permute-start(bf16[256,512]{1,0:T(8,128)(2,1)S(1)} %collective-permute-done.6.refs_10_.refs_9_.refs_3_), channel_id=1, source_target_pairs={{0,1},{1,0},{2,3},{3,2},{4,5},{5,4},{6,7},{7,6},{8,9},{9,8},{10,11... | collective-permute-start | bytes 786440 | tf_op jit(solution)/shard_map/ppermute | solution.py:46
  35.1 1.8 %shard_map.48 = (f32[1024,512]{1,0:T(8,128)S(1)}, f32[1024,128]{1,0:T(8,128)S(1)}, f32[1024,512]{1,0:T(8,128)S(1)}, f32[1024,128]{1,0:T(8,128)S(1)}) custom-call(bf16[512,512]{1,0:T(8,128)(2,1)S(1)} %pad_maximum_fusion.1.refs_0_, ...), custom_call_target="tpu_custom_call", output_to_operand_aliasing={{0}: (12, {}), {1}: (13, {}), {2}: (14, {}), {3}: (15, {})} | custom-call | flops 1073741824 | bytes 524288 | tf_op jit(solution)/shard_map/pallas_call | solution.py:211
  37.1 1.7 %collective-permute-start.19 = (bf16[512,512]{1,0:T(8,128)(2,1)S(1)}, bf16[512,512]{1,0:T(8,128)(2,1)S(1)}, u32[]{:S(2)}, u32[]{:S(2)}) collective-permute-start(bf16[512,512]{1,0:T(8,128)(2,1)S(1)} %slice.14), channel_id=1, source_target_pairs={{0,2},{1,9},{2,4},{3,11},{4,6},{5,13},{6,0},{7,15},{8,10},{9,17},{... | collective-permute-start | bytes 1572872 | tf_op jit(solution)/shard_map/ppermute | solution.py:42
  38.8 6.7 %shard_map.49 = (f32[1024,512]{1,0:T(8,128)S(1)}, f32[1024,128]{1,0:T(8,128)S(1)}, f32[1024,512]{1,0:T(8,128)S(1)}, f32[1024,128]{1,0:T(8,128)S(1)}) custom-call(bf16[1024,512]{1,0:T(8,128)(2,1)S(1)} %collective-permute-done.17.refs_0_, ...), custom_call_target="tpu_custom_call", output_to_operand_aliasing={{0}: (11, {}), {1}: (12, {}), {2}: (13, {}), {3}: (14, {})} | custom-call | flops 5100273664 | bytes 393216 | tf_op jit(solution)/shard_map/pallas_call | solution.py:211
  45.5 1.7 %collective-permute-done.11.refs_0_ = bf16[1024,512]{1,0:T(8,128)(2,1)S(1)} collective-permute-done((bf16[1024,512]{1,0:T(8,128)(2,1)S(1)}, bf16[1024,512]{1,0:T(8,128)(2,1)S(1)}, u32[]{:S(2)}, u32[]{:S(2)}) %collective-permute-start.11) | collective-permute-done | bytes 1048608 | tf_op jit(solution)/shard_map/ppermute | solution.py:42
  47.4 2.7 %collective-permute-start.14 = (bf16[512,512]{1,0:T(8,128)(2,1)S(1)}, bf16[512,512]{1,0:T(8,128)(2,1)S(1)}, u32[]{:S(2)}, u32[]{:S(2)}) collective-permute-start(bf16[512,512]{1,0:T(8,128)(2,1)S(1)} %slice.17), channel_id=1, source_target_pairs={{0,6},{1,25},{2,0},{3,27},{4,2},{5,29},{6,4},{7,31},{8,14},{9,1},{... | collective-permute-start | bytes 1572872 | tf_op jit(solution)/shard_map/ppermute | solution.py:42
  50.1 2.7 %collective-permute-done.19.refs_2_ = bf16[512,512]{1,0:T(8,128)(2,1)S(1)} collective-permute-done((bf16[512,512]{1,0:T(8,128)(2,1)S(1)}, bf16[512,512]{1,0:T(8,128)(2,1)S(1)}, u32[]{:S(2)}, u32[]{:S(2)}) %collective-permute-start.19) | collective-permute-done | bytes 524320 | tf_op jit(solution)/shard_map/ppermute | solution.py:42
  52.8 4.2 %shard_map.52 = bf16[1024,640]{1,0:T(8,128)(2,1)S(1)} custom-call(bf16[1024,512]{1,0:T(8,128)(2,1)S(1)} %collective-permute-done.11.refs_0_, bf16[1024,512]{1,0:T(8,128)(2,1)S(1)} %collective-permute-done.13.refs_1_, bf16[512,512]{1,0:T(8,128)(2,1)S(1)} %collective-permute-done.19.refs_2_, bf16[512,512]{1,0:T(8,128)(2,1)S(1)} %collective-permute-done.21.refs_3_, ...), custom_call_target="tpu_custom_call" | custom-call | flops 9663676416 | bytes 524288 | tf_op jit(solution)/shard_map/pallas_call | solution.py:211
  58.6 2.5 %shard_map.50 = (f32[1024,512]{1,0:T(8,128)S(1)}, f32[1024,128]{1,0:T(8,128)S(1)}) custom-call(bf16[1024,512]{1,0:T(8,128)(2,1)S(1)} %collective-permute-done.11.refs_0_, bf16[1024,512]{1,0:T(8,128)(2,1)S(1)} %collective-permute-done.13.refs_1_, ...), custom_call_target="tpu_custom_call", output_to_operand_aliasing={{0}: (12, {}), {1}: (13, {})} | custom-call | flops 4831838208 | bytes 524288 | tf_op jit(solution)/shard_map/pallas_call | solution.py:211
  61.2 2.5 %shard_map.51 = (f32[1024,512]{1,0:T(8,128)S(1)}, f32[1024,128]{1,0:T(8,128)S(1)}) custom-call(bf16[1024,512]{1,0:T(8,128)(2,1)S(1)} %collective-permute-done.11.refs_0_, bf16[1024,512]{1,0:T(8,128)(2,1)S(1)} %collective-permute-done.13.refs_1_, ...), custom_call_target="tpu_custom_call", output_to_operand_aliasing={{0}: (12, {}), {1}: (13, {})} | custom-call | flops 4831838208 | bytes 524288 | tf_op jit(solution)/shard_map/pallas_call | solution.py:211
  63.7 1.6 %shard_map.53 = (f32[1024,512]{1,0:T(8,128)S(1)}, f32[1024,128]{1,0:T(8,128)S(1)}) custom-call(f32[1024,512]{1,0:T(8,128)S(1)} %get-tuple-element.65.acc, f32[1024,128]{1,0:T(8,128)S(1)} %get-tuple-element.66.ml, bf16[1024,640]{1,0:T(8,128)(2,1)S(1)} %collective-permute-done.22.other), custom_call_target="tpu_custom_call", output_to_operand_aliasing={{0}: (0, {}), {1}: (1, {})} | custom-call | tf_op jit(solution)/shard_map/pallas_call | solution.py:240
  65.3 3.0 %shard_map.54 = (bf16[256,512]{1,0:T(8,128)(2,1)S(1)}, bf16[256,512]{1,0:T(8,128)(2,1)S(1)}, bf16[256,512]{1,0:T(8,128)(2,1)S(1)}, bf16[256,512]{1,0:T(8,128)(2,1)S(1)}) custom-call(bf16[256,512]{1,0:T(8,128)(2,1)S(1)} %get-tuple-element.41.refs_3_.refs_4_.refs_0_, bf16[256,512]{1,0:T(8,128)(2,1)S(1)} %collective-permute-done.2.refs_4_.refs_5_.refs_1_, ...), custom_call_target="tpu_custom_call" | custom-call | tf_op jit(solution)/shard_map/pallas_call | solution.py:272
  68.9 3.3 %collective-permute-start.24 = (bf16[256,512]{1,0:T(8,128)(2,1)S(1)}, bf16[256,512]{1,0:T(8,128)(2,1)S(1)}, u32[]{:S(2)}, u32[]{:S(2)}) collective-permute-start(bf16[256,512]{1,0:T(8,128)(2,1)S(1)} %get-tuple-element.73), channel_id=1, source_target_pairs={{0,64},{32,96},{64,0},{96,32},{1,65},{33,97},{65,1},{97,33},{2,66}... | collective-permute-start | bytes 786440 | tf_op jit(solution)/shard_map/ppermute | solution.py:59
  72.9 1.9 %collective-permute-done.23.r1 = bf16[256,512]{1,0:T(8,128)(2,1)S(1)} collective-permute-done((bf16[256,512]{1,0:T(8,128)(2,1)S(1)}, bf16[256,512]{1,0:T(8,128)(2,1)S(1)}, u32[]{:S(2)}, u32[]{:S(2)}) %collective-permute-start.23) | collective-permute-done | bytes 262176 | tf_op jit(solution)/shard_map/ppermute | solution.py:55
  74.8 7.0 %collective-permute-done.24.r2 = bf16[256,512]{1,0:T(8,128)(2,1)S(1)} collective-permute-done((bf16[256,512]{1,0:T(8,128)(2,1)S(1)}, bf16[256,512]{1,0:T(8,128)(2,1)S(1)}, u32[]{:S(2)}, u32[]{:S(2)}) %collective-permute-start.24) | collective-permute-done | bytes 262176 | tf_op jit(solution)/shard_map/ppermute | solution.py:59
  (50 shorter events, 16.9 us)
Async XLA Ops:
  2.5 9.8 %collective-permute-start.7 = (bf16[512,512]{1,0:T(8,128)(2,1)S(1)}, bf16[512,512]{1,0:T(8,128)(2,1)S(1)}, u32[]{:S(2)}, u32[]{:S(2)}) collective-permute-start(bf16[512,512]{1,0:T(8,128)(2,1)S(1)} %pad_maximum_fusion.1.refs_0_), channel_id=1, source_target_pairs={{0,8},{1,3},{2,10},{3,5},{4,12},{5,7},{6,14},{7,1},{8,16},{9,11},{... | collective-permute-start | bytes 1572872 | tf_op jit(solution)/shard_map/ppermute | solution.py:38
  4.0 8.4 %collective-permute-start.9 = (bf16[512,512]{1,0:T(8,128)(2,1)S(1)}, bf16[512,512]{1,0:T(8,128)(2,1)S(1)}, u32[]{:S(2)}, u32[]{:S(2)}) collective-permute-start(bf16[512,512]{1,0:T(8,128)(2,1)S(1)} %pad_maximum_fusion.1.refs_0_), channel_id=1, source_target_pairs={{0,24},{1,7},{2,26},{3,1},{4,28},{5,3},{6,30},{7,5},{8,0},{9,15},{... | collective-permute-start | bytes 1572872 | tf_op jit(solution)/shard_map/ppermute | solution.py:38
  8.3 7.1 %collective-permute-start.2 = (bf16[256,512]{1,0:T(8,128)(2,1)S(1)}, bf16[256,512]{1,0:T(8,128)(2,1)S(1)}, u32[]{:S(2)}, u32[]{:S(2)}) collective-permute-start(bf16[256,512]{1,0:T(8,128)(2,1)S(1)} %get-tuple-element.42), channel_id=1, source_target_pairs={{0,32},{1,97},{2,34},{3,99},{4,36},{5,101},{6,38},{7,103},{8,40},{... | collective-permute-start | bytes 786440 | tf_op jit(solution)/shard_map/ppermute | solution.py:55
  12.1 6.1 %collective-permute-start.3 = (bf16[256,512]{1,0:T(8,128)(2,1)S(1)}, bf16[256,512]{1,0:T(8,128)(2,1)S(1)}, u32[]{:S(2)}, u32[]{:S(2)}) collective-permute-start(bf16[256,512]{1,0:T(8,128)(2,1)S(1)} %get-tuple-element.43), channel_id=1, source_target_pairs={{0,32},{1,97},{2,34},{3,99},{4,36},{5,101},{6,38},{7,103},{8,40},{... | collective-permute-start | bytes 786440 | tf_op jit(solution)/shard_map/ppermute | solution.py:55
  12.2 8.8 %collective-permute-start.5 = (bf16[256,512]{1,0:T(8,128)(2,1)S(1)}, bf16[256,512]{1,0:T(8,128)(2,1)S(1)}, u32[]{:S(2)}, u32[]{:S(2)}) collective-permute-start(bf16[256,512]{1,0:T(8,128)(2,1)S(1)} %get-tuple-element.44), channel_id=1, source_target_pairs={{0,32},{1,97},{2,34},{3,99},{4,36},{5,101},{6,38},{7,103},{8,40},{... | collective-permute-start | bytes 786440 | tf_op jit(solution)/shard_map/ppermute | solution.py:55
  12.3 15.9 %collective-permute-start.8 = (bf16[512,512]{1,0:T(8,128)(2,1)S(1)}, bf16[512,512]{1,0:T(8,128)(2,1)S(1)}, u32[]{:S(2)}, u32[]{:S(2)}) collective-permute-start(bf16[512,512]{1,0:T(8,128)(2,1)S(1)} %collective-permute-done.7.refs_1_), channel_id=1, source_target_pairs={{0,8},{1,3},{2,10},{3,5},{4,12},{5,7},{6,14},{7,1},{8,16},{9,11},{... | collective-permute-start | bytes 1572872 | tf_op jit(solution)/shard_map/ppermute | solution.py:38
  12.4 24.5 %collective-permute-start.20 = (bf16[1024,512]{1,0:T(8,128)(2,1)S(1)}, bf16[1024,512]{1,0:T(8,128)(2,1)S(1)}, u32[]{:S(2)}, u32[]{:S(2)}) collective-permute-start(bf16[1024,512]{1,0:T(8,128)(2,1)S(1)} %pad_maximum_fusion), channel_id=1, source_target_pairs={{0,6},{1,25},{2,0},{3,27},{4,2},{5,29},{6,4},{7,31},{8,14},{9,1},{... | collective-permute-start | bytes 3145736 | tf_op jit(solution)/shard_map/ppermute | solution.py:42
  15.4 21.5 %collective-permute-start.17 = (bf16[1024,512]{1,0:T(8,128)(2,1)S(1)}, bf16[1024,512]{1,0:T(8,128)(2,1)S(1)}, u32[]{:S(2)}, u32[]{:S(2)}) collective-permute-start(bf16[1024,512]{1,0:T(8,128)(2,1)S(1)} %pad_maximum_fusion), channel_id=1, source_target_pairs={{0,2},{1,9},{2,4},{3,11},{4,6},{5,13},{6,0},{7,15},{8,10},{9,17},{... | collective-permute-start | bytes 3145736 | tf_op jit(solution)/shard_map/ppermute | solution.py:42
  18.2 5.1 %collective-permute-start.10 = (bf16[256,512]{1,0:T(8,128)(2,1)S(1)}, bf16[256,512]{1,0:T(8,128)(2,1)S(1)}, u32[]{:S(2)}, u32[]{:S(2)}) collective-permute-start(bf16[256,512]{1,0:T(8,128)(2,1)S(1)} %collective-permute-done.2.refs_4_.refs_5_.refs_1_), channel_id=1, source_target_pairs={{0,1},{1,0},{2,3},{3,2},{4,5},{5,4},{6,7},{7,6},{8,9},{9,8},{10,11... | collective-permute-start | bytes 786440 | tf_op jit(solution)/shard_map/ppermute | solution.py:46
  21.0 4.1 %collective-permute-start.4 = (bf16[256,512]{1,0:T(8,128)(2,1)S(1)}, bf16[256,512]{1,0:T(8,128)(2,1)S(1)}, u32[]{:S(2)}, u32[]{:S(2)}) collective-permute-start(bf16[256,512]{1,0:T(8,128)(2,1)S(1)} %collective-permute-done.3.refs_5_.refs_6_), channel_id=1, source_target_pairs={{0,1},{1,0},{2,3},{3,2},{4,5},{5,4},{6,7},{7,6},{8,9},{9,8},{10,11... | collective-permute-start | bytes 786440 | tf_op jit(solution)/shard_map/ppermute | solution.py:46
  23.3 7.7 %collective-permute-start.6 = (bf16[256,512]{1,0:T(8,128)(2,1)S(1)}, bf16[256,512]{1,0:T(8,128)(2,1)S(1)}, u32[]{:S(2)}, u32[]{:S(2)}) collective-permute-start(bf16[256,512]{1,0:T(8,128)(2,1)S(1)} %collective-permute-done.5), channel_id=1, source_target_pairs={{0,32},{1,97},{2,34},{3,99},{4,36},{5,101},{6,38},{7,103},{8,40},{... | collective-permute-start | bytes 786440 | tf_op jit(solution)/shard_map/ppermute | solution.py:55
  28.2 18.9 %collective-permute-start.11 = (bf16[1024,512]{1,0:T(8,128)(2,1)S(1)}, bf16[1024,512]{1,0:T(8,128)(2,1)S(1)}, u32[]{:S(2)}, u32[]{:S(2)}) collective-permute-start(bf16[1024,512]{1,0:T(8,128)(2,1)S(1)} %constant_dynamic-update-slice_fusion), channel_id=1, source_target_pairs={{0,2},{1,9},{2,4},{3,11},{4,6},{5,13},{6,0},{7,15},{8,10},{9,17},{... | collective-permute-start | bytes 3145736 | tf_op jit(solution)/shard_map/ppermute | solution.py:42
  28.6 18.7 %collective-permute-start.13 = (bf16[1024,512]{1,0:T(8,128)(2,1)S(1)}, bf16[1024,512]{1,0:T(8,128)(2,1)S(1)}, u32[]{:S(2)}, u32[]{:S(2)}) collective-permute-start(bf16[1024,512]{1,0:T(8,128)(2,1)S(1)} %constant_dynamic-update-slice_fusion), channel_id=1, source_target_pairs={{0,6},{1,25},{2,0},{3,27},{4,2},{5,29},{6,4},{7,31},{8,14},{9,1},{... | collective-permute-start | bytes 3145736 | tf_op jit(solution)/shard_map/ppermute | solution.py:42
  31.0 4.1 %collective-permute-start.18 = (bf16[256,512]{1,0:T(8,128)(2,1)S(1)}, bf16[256,512]{1,0:T(8,128)(2,1)S(1)}, u32[]{:S(2)}, u32[]{:S(2)}) collective-permute-start(bf16[256,512]{1,0:T(8,128)(2,1)S(1)} %collective-permute-done.6.refs_10_.refs_9_.refs_3_), channel_id=1, source_target_pairs={{0,1},{1,0},{2,3},{3,2},{4,5},{5,4},{6,7},{7,6},{8,9},{9,8},{10,11... | collective-permute-start | bytes 786440 | tf_op jit(solution)/shard_map/ppermute | solution.py:46
  37.0 13.1 %collective-permute-start.21 = (bf16[512,512]{1,0:T(8,128)(2,1)S(1)}, bf16[512,512]{1,0:T(8,128)(2,1)S(1)}, u32[]{:S(2)}, u32[]{:S(2)}) collective-permute-start(bf16[512,512]{1,0:T(8,128)(2,1)S(1)} %slice.15), channel_id=1, source_target_pairs={{0,6},{1,25},{2,0},{3,27},{4,2},{5,29},{6,4},{7,31},{8,14},{9,1},{... | collective-permute-start | bytes 1572872 | tf_op jit(solution)/shard_map/ppermute | solution.py:42
  37.1 15.7 %collective-permute-start.19 = (bf16[512,512]{1,0:T(8,128)(2,1)S(1)}, bf16[512,512]{1,0:T(8,128)(2,1)S(1)}, u32[]{:S(2)}, u32[]{:S(2)}) collective-permute-start(bf16[512,512]{1,0:T(8,128)(2,1)S(1)} %slice.14), channel_id=1, source_target_pairs={{0,2},{1,9},{2,4},{3,11},{4,6},{5,13},{6,0},{7,15},{8,10},{9,17},{... | collective-permute-start | bytes 1572872 | tf_op jit(solution)/shard_map/ppermute | solution.py:42
  47.2 10.9 %collective-permute-start.12 = (bf16[512,512]{1,0:T(8,128)(2,1)S(1)}, bf16[512,512]{1,0:T(8,128)(2,1)S(1)}, u32[]{:S(2)}, u32[]{:S(2)}) collective-permute-start(bf16[512,512]{1,0:T(8,128)(2,1)S(1)} %slice.16), channel_id=1, source_target_pairs={{0,2},{1,9},{2,4},{3,11},{4,6},{5,13},{6,0},{7,15},{8,10},{9,17},{... | collective-permute-start | bytes 1572872 | tf_op jit(solution)/shard_map/ppermute | solution.py:42
  47.4 10.8 %collective-permute-start.14 = (bf16[512,512]{1,0:T(8,128)(2,1)S(1)}, bf16[512,512]{1,0:T(8,128)(2,1)S(1)}, u32[]{:S(2)}, u32[]{:S(2)}) collective-permute-start(bf16[512,512]{1,0:T(8,128)(2,1)S(1)} %slice.17), channel_id=1, source_target_pairs={{0,6},{1,25},{2,0},{3,27},{4,2},{5,29},{6,4},{7,31},{8,14},{9,1},{... | collective-permute-start | bytes 1572872 | tf_op jit(solution)/shard_map/ppermute | solution.py:42
  57.1 6.6 %collective-permute-start.22 = (bf16[1024,640]{1,0:T(8,128)(2,1)S(1)}, bf16[1024,640]{1,0:T(8,128)(2,1)S(1)}, u32[]{:S(2)}, u32[]{:S(2)}) collective-permute-start(bf16[1024,640]{1,0:T(8,128)(2,1)S(1)} %shard_map.52), channel_id=1, source_target_pairs={{0,1},{1,0},{2,3},{3,2},{4,5},{5,4},{6,7},{7,6},{8,9},{9,8},{10,11... | collective-permute-start | bytes 3932168 | tf_op jit(solution)/shard_map/ppermute | solution.py:46
  58.1 7.2 %collective-permute-start.15 = (bf16[512,512]{1,0:T(8,128)(2,1)S(1)}, bf16[512,512]{1,0:T(8,128)(2,1)S(1)}, u32[]{:S(2)}, u32[]{:S(2)}) collective-permute-start(bf16[512,512]{1,0:T(8,128)(2,1)S(1)} %collective-permute-done.12.refs_4_), channel_id=1, source_target_pairs={{0,1},{1,0},{2,3},{3,2},{4,5},{5,4},{6,7},{7,6},{8,9},{9,8},{10,11... | collective-permute-start | bytes 1572872 | tf_op jit(solution)/shard_map/ppermute | solution.py:46
  58.1 7.2 %collective-permute-start.16 = (bf16[512,512]{1,0:T(8,128)(2,1)S(1)}, bf16[512,512]{1,0:T(8,128)(2,1)S(1)}, u32[]{:S(2)}, u32[]{:S(2)}) collective-permute-start(bf16[512,512]{1,0:T(8,128)(2,1)S(1)} %collective-permute-done.14.refs_5_), channel_id=1, source_target_pairs={{0,1},{1,0},{2,3},{3,2},{4,5},{5,4},{6,7},{7,6},{8,9},{9,8},{10,11... | collective-permute-start | bytes 1572872 | tf_op jit(solution)/shard_map/ppermute | solution.py:46
  68.3 6.5 %collective-permute-start.23 = (bf16[256,512]{1,0:T(8,128)(2,1)S(1)}, bf16[256,512]{1,0:T(8,128)(2,1)S(1)}, u32[]{:S(2)}, u32[]{:S(2)}) collective-permute-start(bf16[256,512]{1,0:T(8,128)(2,1)S(1)} %get-tuple-element.72), channel_id=1, source_target_pairs={{0,96},{1,33},{2,98},{3,35},{4,100},{5,37},{6,102},{7,39},{8,104},... | collective-permute-start | bytes 786440 | tf_op jit(solution)/shard_map/ppermute | solution.py:55
  68.9 12.9 %collective-permute-start.24 = (bf16[256,512]{1,0:T(8,128)(2,1)S(1)}, bf16[256,512]{1,0:T(8,128)(2,1)S(1)}, u32[]{:S(2)}, u32[]{:S(2)}) collective-permute-start(bf16[256,512]{1,0:T(8,128)(2,1)S(1)} %get-tuple-element.73), channel_id=1, source_target_pairs={{0,64},{32,96},{64,0},{96,32},{1,65},{33,97},{65,1},{97,33},{2,66}... | collective-permute-start | bytes 786440 | tf_op jit(solution)/shard_map/ppermute | solution.py:59
  72.2 11.0 %collective-permute-start.25 = (bf16[256,512]{1,0:T(8,128)(2,1)S(1)}, bf16[256,512]{1,0:T(8,128)(2,1)S(1)}, u32[]{:S(2)}, u32[]{:S(2)}) collective-permute-start(bf16[256,512]{1,0:T(8,128)(2,1)S(1)} %get-tuple-element.74), channel_id=1, source_target_pairs={{0,32},{1,97},{2,34},{3,99},{4,36},{5,101},{6,38},{7,103},{8,40},{... | collective-permute-start | bytes 786440 | tf_op jit(solution)/shard_map/ppermute | solution.py:55
  (4 other events, 8.3 us)
